TPU v7x, 32 devices: a whole 2x2x4 slice. The times are simulated.
32 devices in a mesh: grp: 4 (over z), sp: 8 (over y, x, core).
Axes of the slice: x: 2, y: 2, z: 4, core: 2. Of those that a mesh axis runs over, the one named last changes fastest.
Arguments:
- q_src: bfloat16 [128, 4, 8, 4096], P(None, 'grp', 'sp'), may hold values from -4.5 to 4.5
- k_src: bfloat16 [128, 4, 8, 1024], P(None, 'grp', 'sp'), may hold values from -4.5 to 4.5
- v_src: bfloat16 [128, 4, 8, 1024], P(None, 'grp', 'sp'), may hold values from -4.5 to 4.5
- grad_src: bfloat16 [128, 4, 8, 4096], P(None, 'grp', 'sp'), may hold values from -4.5 to 4.5
- doc_lengths: int32 [192], replicated, may hold values from 0 to 5, as said below
- doc_groups: int32 [192], replicated, may hold values from 0 to 3, as said below
- doc_offsets: int32 [192], replicated, may hold values from 0 to 47, as said below
Outputs:
- dq_grp: bfloat16 [4, 192, 8, 4096], P('grp', None, 'sp')
- dk_grp: bfloat16 [4, 192, 8, 1024], P('grp', None, 'sp')
- dv_grp: bfloat16 [4, 192, 8, 1024], P('grp', None, 'sp')
Inputs may be any that keep to these rules, and one draw needn't show every extreme that they name: `doc_lengths`: documents of positive length come first, absent ones (length 0) last; the lengths sum to 128 and one document has exactly 5 blocks. `doc_groups`: placed at their offsets, the documents of a group cover its blocks 0 up to its total without gaps or intersection; every group receives at least one block, none more than 48, and one group exactly 48. Absent documents name group 0. `doc_offsets`: absent documents have offset 0.
All inputs are finite; a program needn't handle non-finite values.
Results may differ from a plain program's by a relative error of at most 0.0091.
Values may be sent and summed in bfloat16 or wider, within the bound.
A program may use at most 64 MiB of HBM per device.

v0:
```python
import math

import jax
import jax.numpy as jnp
from jax import lax
from jax.sharding import PartitionSpec as P

HEADS = 32
KV_HEADS = 8
HEAD_DIM = 128


NEG_FILL = -1e30


def unchanged(passed):
    return passed


def collapse(array):
    rounded = lax.optimization_barrier(array)
    return jnp.sum(rounded.astype(jnp.float32), axis=2)


def pair_fold(low_part, high_part):
    return lax.optimization_barrier(
        (low_part.astype(jnp.float32) + high_part.astype(jnp.float32)).astype(jnp.bfloat16)
    )


def halves_total(array):
    half = array.shape[2] // 2
    return collapse(pair_fold(array[:, :, :half], array[:, :, half:]))


def attend(q_heads, k_heads, v_heads, g_heads, first_tok):
    tokens_here, kv_local, q_per_kv, head_dim = q_heads.shape
    span_len = math.gcd(tokens_here, 512)
    blocks = tokens_here // span_len
    factor = head_dim ** (-0.5)
    lane_pos = jnp.arange(span_len, dtype=jnp.int32)
    block_low = jnp.min(first_tok.reshape(blocks, span_len), axis=1)
    heads_shape = (kv_local, q_per_kv, span_len)

    def cut_block(array, index):
        return lax.dynamic_slice_in_dim(array, index * span_len, span_len, 0)

    def pair_logits(q_block, first_q, q_index, k_index):
        k_block = cut_block(k_heads, k_index)
        logits = (
            jnp.einsum("qjih,kjh->jiqk", q_block, k_block, preferred_element_type=jnp.float32)
            * factor
        )
        q_pos = q_index * span_len + lane_pos
        k_pos = k_index * span_len + lane_pos
        allowed = (k_pos[None, :] <= q_pos[:, None]) & (k_pos[None, :] >= first_q[:, None])
        return (logits, allowed)

    def is_live(q_index, k_index):
        return block_low[q_index] <= k_index * span_len + span_len - 1

    def row_norm(q_index):
        q_block = cut_block(q_heads, q_index)
        first_q = cut_block(first_tok, q_index)

        def visit_key(k_index, running):

            def update(running):
                row_high, row_mass = running
                logits, allowed = pair_logits(q_block, first_q, q_index, k_index)
                logits = jnp.where(allowed, logits, NEG_FILL)
                new_high = jnp.maximum(row_high, jnp.max(logits, axis=-1))
                row_mass = row_mass * jnp.exp(row_high - new_high) + jnp.sum(
                    jnp.where(allowed, jnp.exp(logits - new_high[..., None]), 0.0), axis=-1
                )
                return (new_high, row_mass)

            return lax.cond(is_live(q_index, k_index), update, unchanged, running)

        initial = (
            jnp.full(heads_shape, NEG_FILL, jnp.float32),
            jnp.zeros(heads_shape, jnp.float32),
        )
        row_high, row_mass = lax.fori_loop(0, q_index + 1, visit_key, initial)
        return row_high + jnp.log(row_mass)

    log_norm = lax.map(row_norm, jnp.arange(blocks, dtype=jnp.int32))

    def row_delta(q_index):
        q_block = cut_block(q_heads, q_index)
        first_q = cut_block(first_tok, q_index)
        norm_row = log_norm[q_index]

        def visit_key(k_index, acc_out):

            def update(acc_out):
                logits, allowed = pair_logits(q_block, first_q, q_index, k_index)
                weights = jnp.where(allowed, jnp.exp(logits - norm_row[..., None]), 0.0).astype(
                    jnp.bfloat16
                )
                v_block = cut_block(v_heads, k_index)
                return acc_out + jnp.einsum(
                    "jiqk,kjh->jiqh", weights, v_block, preferred_element_type=jnp.float32
                )

            return lax.cond(is_live(q_index, k_index), update, unchanged, acc_out)

        acc_out = lax.fori_loop(
            0, q_index + 1, visit_key, jnp.zeros(heads_shape + (head_dim,), jnp.float32)
        )
        g_block = cut_block(g_heads, q_index)
        return jnp.einsum("jiqh,qjih->jiq", acc_out, g_block, preferred_element_type=jnp.float32)

    delta_all = lax.map(row_delta, jnp.arange(blocks, dtype=jnp.int32))

    def back_row(q_index, carried):
        grad_q, grad_k, grad_v = carried
        q_block = cut_block(q_heads, q_index)
        g_block = cut_block(g_heads, q_index)
        first_q = cut_block(first_tok, q_index)
        norm_row = log_norm[q_index]
        delta_row = delta_all[q_index]

        def visit_key(k_index, inner):

            def update(inner):
                q_acc, grad_k, grad_v = inner
                logits, allowed = pair_logits(q_block, first_q, q_index, k_index)
                probs = jnp.where(allowed, jnp.exp(logits - norm_row[..., None]), 0.0)
                probs_low = probs.astype(jnp.bfloat16)
                k_block = cut_block(k_heads, k_index)
                v_block = cut_block(v_heads, k_index)
                d_probs = jnp.einsum(
                    "qjih,kjh->jiqk", g_block, v_block, preferred_element_type=jnp.float32
                )
                d_logits = (probs * (d_probs - delta_row[..., None])).astype(jnp.bfloat16)
                q_acc = q_acc + jnp.einsum(
                    "jiqk,kjh->qjih", d_logits, k_block, preferred_element_type=jnp.float32
                )
                k_part = jnp.einsum(
                    "jiqk,qjih->kjih", d_logits, q_block, preferred_element_type=jnp.float32
                )
                v_part = jnp.einsum(
                    "jiqk,qjih->kjih", probs_low, g_block, preferred_element_type=jnp.float32
                )
                at_row = k_index * span_len
                grad_k = lax.dynamic_update_slice_in_dim(
                    grad_k, cut_block(grad_k, k_index) + k_part, at_row, 0
                )
                grad_v = lax.dynamic_update_slice_in_dim(
                    grad_v, cut_block(grad_v, k_index) + v_part, at_row, 0
                )
                return (q_acc, grad_k, grad_v)

            return lax.cond(is_live(q_index, k_index), update, unchanged, inner)

        q_start = jnp.zeros((span_len, kv_local, q_per_kv, head_dim), jnp.float32)
        q_acc, grad_k, grad_v = lax.fori_loop(0, q_index + 1, visit_key, (q_start, grad_k, grad_v))
        grad_q = lax.dynamic_update_slice_in_dim(grad_q, q_acc, q_index * span_len, 0)
        return (grad_q, grad_k, grad_v)

    empty = jnp.zeros((tokens_here, kv_local, q_per_kv, head_dim), jnp.float32)
    grad_q, grad_k, grad_v = lax.fori_loop(0, blocks, back_row, (empty, empty, empty))
    return (grad_q * factor, grad_k * factor, grad_v)


def on_device(q_src, k_src, v_src, grad_src, doc_lengths, doc_groups, doc_offsets):
    grp_count = lax.axis_size("grp")
    sp_count = lax.axis_size("sp")
    unit_count = q_src.shape[0]
    slot_count = doc_lengths.shape[0]
    group_cap = slot_count // grp_count
    row_count = group_cap * grp_count
    unit_tok = grp_count * sp_count
    group_tok = row_count * sp_count
    head_dim = HEAD_DIM
    copies = max(1, sp_count // KV_HEADS)
    kv_local = max(1, KV_HEADS // sp_count)
    q_local = HEADS // sp_count
    q_per_kv = q_local // kv_local
    unit_ids = jnp.arange(unit_count, dtype=jnp.int32)
    starts = jnp.cumsum(doc_lengths) - doc_lengths
    inside = (
        (unit_ids[:, None] >= starts[None, :])
        & (unit_ids[:, None] < (starts + doc_lengths)[None, :])
    ).astype(jnp.int32)
    group_of = jnp.sum(inside * doc_groups[None, :], axis=1)
    place_of = jnp.sum(
        inside * (doc_offsets[None, :] + unit_ids[:, None] - starts[None, :]), axis=1
    )
    slot_of = group_of * group_cap + place_of
    slot_ids = jnp.arange(row_count, dtype=jnp.int32).reshape(grp_count, group_cap).T.reshape(-1)
    matches = (slot_of[None, :] == slot_ids[:, None]).astype(jnp.int32)
    source = jnp.sum(matches * unit_ids[None, :], axis=1)
    filled = jnp.sum(matches, axis=1) > 0

    def pack_rows(array):
        flat = array.reshape(unit_count, array.shape[-1])
        picked = jnp.take(flat, source, axis=0)
        picked = jnp.where(filled[:, None], picked, jnp.zeros_like(picked))
        return picked.reshape(group_cap, grp_count, array.shape[-1])

    arrived = (
        lax.all_to_all(pack_rows(q_src), "grp", split_axis=1, concat_axis=1, tiled=True),
        lax.all_to_all(pack_rows(k_src), "grp", split_axis=1, concat_axis=1, tiled=True),
        lax.all_to_all(pack_rows(v_src), "grp", split_axis=1, concat_axis=1, tiled=True),
        lax.all_to_all(pack_rows(grad_src), "grp", split_axis=1, concat_axis=1, tiled=True),
    )
    q_rows = arrived[0].reshape(row_count, 1, HEADS, head_dim)
    k_rows = arrived[1].reshape(row_count, KV_HEADS, head_dim)
    v_rows = arrived[2].reshape(row_count, KV_HEADS, head_dim)
    g_rows = arrived[3].reshape(row_count, 1, HEADS, head_dim)
    my_group = lax.axis_index("grp")
    unit_place = jnp.arange(group_cap, dtype=jnp.int32)
    member = (
        (doc_groups[None, :] == my_group)
        & (doc_lengths[None, :] > 0)
        & (doc_offsets[None, :] <= unit_place[:, None])
        & (unit_place[:, None] < (doc_offsets + doc_lengths)[None, :])
    ).astype(jnp.int32)
    first_unit = jnp.sum(member * doc_offsets[None, :], axis=1)
    occupied = jnp.sum(member, axis=1) > 0
    token_ids = jnp.arange(group_tok, dtype=jnp.int32)
    first_tok = jnp.where(
        jnp.repeat(occupied, unit_tok), jnp.repeat(first_unit * unit_tok, unit_tok), token_ids
    )
    k_wide = jnp.repeat(k_rows, copies, axis=1).reshape(row_count, 1, KV_HEADS * copies, head_dim)
    v_wide = jnp.repeat(v_rows, copies, axis=1).reshape(row_count, 1, KV_HEADS * copies, head_dim)
    q_back, g_back, k_back, v_back = (
        lax.all_to_all(q_rows, "sp", split_axis=2, concat_axis=1, tiled=True),
        lax.all_to_all(g_rows, "sp", split_axis=2, concat_axis=1, tiled=True),
        lax.all_to_all(k_wide, "sp", split_axis=2, concat_axis=1, tiled=True),
        lax.all_to_all(v_wide, "sp", split_axis=2, concat_axis=1, tiled=True),
    )
    k_heads = k_back.reshape(group_tok, kv_local, head_dim)
    v_heads = v_back.reshape(group_tok, kv_local, head_dim)
    q_heads = q_back.reshape(group_tok, kv_local, q_per_kv, head_dim)
    g_heads = g_back.reshape(group_tok, kv_local, q_per_kv, head_dim)
    grad_q, grad_k, grad_v = attend(q_heads, k_heads, v_heads, g_heads, first_tok)
    q_low = grad_q.astype(jnp.bfloat16).reshape(row_count, sp_count, q_local, head_dim)
    k_low = grad_k.astype(jnp.bfloat16)
    v_low = grad_v.astype(jnp.bfloat16)
    q_home, k_home, v_home = (
        lax.all_to_all(q_low, "sp", split_axis=1, concat_axis=2, tiled=True),
        lax.all_to_all(
            k_low.reshape(row_count, sp_count, q_local, head_dim),
            "sp",
            split_axis=1,
            concat_axis=2,
            tiled=True,
        ),
        lax.all_to_all(
            v_low.reshape(row_count, sp_count, q_local, head_dim),
            "sp",
            split_axis=1,
            concat_axis=2,
            tiled=True,
        ),
    )
    k_sum = halves_total(k_home.reshape(row_count, KV_HEADS, HEADS // KV_HEADS, head_dim))
    v_sum = halves_total(v_home.reshape(row_count, KV_HEADS, HEADS // KV_HEADS, head_dim))
    dk_out = k_sum.astype(jnp.bfloat16).reshape(1, row_count, 1, KV_HEADS * head_dim)
    dv_out = v_sum.astype(jnp.bfloat16).reshape(1, row_count, 1, KV_HEADS * head_dim)
    dq_out = q_home.reshape(1, row_count, 1, HEADS * head_dim)
    return (dq_out, dk_out, dv_out)


def solution(mesh):
    placed = (
        P(None, "grp", "sp", None),
        P(None, "grp", "sp", None),
        P(None, "grp", "sp", None),
        P(None, "grp", "sp", None),
        P(),
        P(),
        P(),
    )
    return jax.shard_map(
        on_device,
        mesh=mesh,
        in_specs=placed,
        out_specs=(
            P("grp", None, "sp", None),
            P("grp", None, "sp", None),
            P("grp", None, "sp", None),
        ),
        check_vma=False,
    )
```

profile of v0, /device:TPU:24, one launch (start us, length us, event | category | flops | bytes accessed | tf_op | source)
XLA Modules:
  0.0 410.4 jit_solution(1183689676402597836)
XLA Ops:
  8.6 5.1 %all-to-all-start.2 = ((bf16[48,4,1024]{2,0,1:T(8,128)(2,1)}), bf16[48,4,1024]{2,0,1:T(8,128)(2,1)S(1)}, u32[]{:S(2)}, u32[]{:S(2)}) async-start(bf16[48,4,1024]{2,0,1:T(8,128)(2,1)} %copy.149), calls=%async_computation.2 | async-start | bytes 786432 | tf_op jit(solution)/shard_map/all_to_all | solution.py:205
  14.7 8.3 %all-to-all-done.2 = bf16[48,4,1024]{2,0,1:T(8,128)(2,1)S(1)} async-done(((bf16[48,4,1024]{2,0,1:T(8,128)(2,1)}), bf16[48,4,1024]{2,0,1:T(8,128)(2,1)S(1)}, u32[]{:S(2)}, u32[]{:S(2)}) %all-to-all-start.2) | async-done | bytes 393248 | tf_op jit(solution)/shard_map/all_to_all | solution.py:205
  23.0 5.8 %all-to-all-start.6 = ((bf16[48,4,1024]{2,0,1:T(8,128)(2,1)}), bf16[48,4,1024]{2,0,1:T(8,128)(2,1)S(1)}, u32[]{:S(2)}, u32[]{:S(2)}) async-start(bf16[48,4,1024]{2,0,1:T(8,128)(2,1)} %copy.158), calls=%async_computation.6 | async-start | bytes 786432 | tf_op jit(solution)/shard_map/all_to_all | solution.py:206
  30.0 7.3 %all-to-all-done.6 = bf16[48,4,1024]{2,0,1:T(8,128)(2,1)S(1)} async-done(((bf16[48,4,1024]{2,0,1:T(8,128)(2,1)}), bf16[48,4,1024]{2,0,1:T(8,128)(2,1)S(1)}, u32[]{:S(2)}, u32[]{:S(2)}) %all-to-all-start.6) | async-done | bytes 393248 | tf_op jit(solution)/shard_map/all_to_all | solution.py:206
  61.1 5.9 %all-to-all-start = ((bf16[48,4,4096]{2,0,1:T(8,128)(2,1)}), bf16[48,4,4096]{2,0,1:T(8,128)(2,1)S(1)}, u32[]{:S(2)}, u32[]{:S(2)}) async-start(bf16[48,4,4096]{2,0,1:T(8,128)(2,1)} %copy.145), calls=%async_computation | async-start | bytes 3145728 | tf_op jit(solution)/shard_map/all_to_all | solution.py:204
  74.1 28.1 %all-to-all-done = bf16[48,4,4096]{2,0,1:T(8,128)(2,1)S(1)} async-done(((bf16[48,4,4096]{2,0,1:T(8,128)(2,1)}), bf16[48,4,4096]{2,0,1:T(8,128)(2,1)S(1)}, u32[]{:S(2)}, u32[]{:S(2)}) %all-to-all-start) | async-done | bytes 1572896 | tf_op jit(solution)/shard_map/all_to_all | solution.py:204
  103.3 5.9 %all-to-all-start.4 = ((bf16[48,4,4096]{2,0,1:T(8,128)(2,1)}), bf16[48,4,4096]{2,0,1:T(8,128)(2,1)S(1)}, u32[]{:S(2)}, u32[]{:S(2)}) async-start(bf16[48,4,4096]{2,0,1:T(8,128)(2,1)} %copy.154), calls=%async_computation.4 | async-start | bytes 3145728 | tf_op jit(solution)/shard_map/all_to_all | solution.py:207
  120.3 23.2 %all-to-all-done.4 = bf16[48,4,4096]{2,0,1:T(8,128)(2,1)S(1)} async-done(((bf16[48,4,4096]{2,0,1:T(8,128)(2,1)}), bf16[48,4,4096]{2,0,1:T(8,128)(2,1)S(1)}, u32[]{:S(2)}, u32[]{:S(2)}) %all-to-all-start.4) | async-done | bytes 1572896 | tf_op jit(solution)/shard_map/all_to_all | solution.py:207
  160.3 9.4 %all-to-all-done.1 = bf16[192,1,32,128]{3,0,1,2:T(8,128)(2,1)S(1)} async-done(((bf16[192,1,32,128]{3,0,1,2:T(8,128)(2,1)}), bf16[192,1,32,128]{3,0,1,2:T(8,128)(2,1)S(1)}, u32[]{:S(2)}, u32[]{:S(2)}) %all-to-all-start.1) | async-done | bytes 1572896 | tf_op jit(solution)/shard_map/all_to_all | solution.py:230
  179.1 31.8 %while.174 = (s32[]{:T(128)}, f32[3,1,4,512]{3,2,1,0:T(4,128)S(1)}, s32[3]{0:T(128)S(1)}, bf16[1536,1,4,128]{3,0,2,1:T(8,128)(2,1)}, s32[1536]{0:T(1024)S(1)}, /...) while((s32[]{:T(128)}, f32[3,1,4,512]{3,2,1,0:T(4,128)S(1)}, ...), condition=%wide.region_17.20_spmd.clone.clone, body=%wide.region_10.19_spmd.clone.clone.sunk | while | flops 277617664 | bytes 11047662 | solution.py:87
  203.3 7.5 %while.179 = (s32[]{:T(128)}, f32[1,4,512]{2,1,0:T(4,128)S(1)}, f32[1,4,512]{2,1,0:T(4,128)S(1)}, s32[]{:T(128)}, s32[1]{0:T(128)}, /*index=5*/s32[512]{0:T(512)...) while((s32[]{:T(128)}, f32[1,4,512]{2,1,0:T(4,128)S(1)}, ...), condition=%wide.region_16.18_spmd.clone, body=%wide.region_11.17_spmd.clone.sunk | while | flops 277615616 | bytes 9951577 | solution.py:84
  213.0 38.9 %while.176 = (s32[]{:T(128)}, f32[3,1,4,512]{3,2,1,0:T(4,128)S(1)}, s32[3]{0:T(128)S(1)}, bf16[1536,1,4,128]{3,0,2,1:T(8,128)(2,1)}, s32[1536]{0:T(1024)S(1)}, /...) while((s32[]{:T(128)}, f32[3,1,4,512]{3,2,1,0:T(4,128)S(1)}, ...), condition=%wide.region_23.26_spmd.clone.clone, body=%wide.region_18.25_spmd.clone.clone.sunk | while | flops 542899200 | bytes 7165686 | solution.py:114
  242.5 7.4 %while.180 = (s32[]{:T(128)}, f32[1,4,512,128]{3,2,1,0:T(8,128)S(1)}, s32[]{:T(128)}, s32[1]{0:T(128)}, s32[512]{0:T(512)S(1)}, /*index=5*/s32[]{:T(128)}, s32[5...) while((s32[]{:T(128)}, ...), condition=%wide.region_22.24_spmd.clone, body=%wide.region_19.23_spmd.clone.sunk | while | flops 542114816 | bytes 3431749 | solution.py:108
  257.8 69.2 %while.178 = (s32[]{:T(128)}, f32[1536,1,4,128]{3,0,2,1:T(8,128)}, f32[1536,1,4,128]{3,0,2,1:T(8,128)}, f32[1536,1,4,128]{3,0,2,1:T(8,128)}, bf16[1536,1,4,128]{...) while((s32[]{:T(128)}, f32[1536,1,4,128]{3,0,2,1:T(8,128)}, ...), condition=%wide.region_29.32_spmd.clone.clone, body=%wide.region_24.31_spmd.clone.clone.sunk | while | flops 1354236928 | bytes 104018936 | solution.py:163
  261.0 13.5 %while.181 = (s32[]{:T(128)}, f32[512,1,4,128]{0,3,2,1:T(8,128)S(1)}, f32[1536,1,4,128]{3,0,2,1:T(8,128)}, f32[1536,1,4,128]{3,0,2,1:T(8,128)}, s32[]{:T(128)}, ...) while((s32[]{:T(128)}, ...), condition=%wide.region_28.30_spmd.clone, body=%wide.region_25.29_spmd.clone.sunk | while | flops 1354236928 | bytes 95591000 | solution.py:158
  261.7 12.8 %conditional.9 = ((f32[512,1,4,128]{0,3,2,1:T(8,128)S(1)}, f32[1536,1,4,128]{3,0,2,1:T(8,128)}, f32[1536,1,4,128]{3,0,2,1:T(8,128)})) conditional(s32[]{:T(128)} %convert_element_type.125, (f32[512,1,4,128]{0,3,2,1:T(8,128)S(1)}, f32[1536,1,4,128]{3,0,2,1:T(8,128)}, f32[1536,1,4,128]{3,0,2,1:T(8,128)}) %tuple.329, (s32[]{:T(128)}, ...), branch_computations={%region_26.27_spmd, %region_27.28_spmd} | conditional | flops 1354236928 | bytes 95590664 | solution.py:155
  279.2 14.1 %while.181 = (s32[]{:T(128)}, f32[512,1,4,128]{0,3,2,1:T(8,128)S(1)}, f32[1536,1,4,128]{3,0,2,1:T(8,128)}, f32[1536,1,4,128]{3,0,2,1:T(8,128)}, s32[]{:T(128)}, ...) while((s32[]{:T(128)}, ...), condition=%wide.region_28.30_spmd.clone, body=%wide.region_25.29_spmd.clone.sunk | while | flops 1354236928 | bytes 95591000 | solution.py:158
  280.5 12.8 %conditional.9 = ((f32[512,1,4,128]{0,3,2,1:T(8,128)S(1)}, f32[1536,1,4,128]{3,0,2,1:T(8,128)}, f32[1536,1,4,128]{3,0,2,1:T(8,128)})) conditional(s32[]{:T(128)} %convert_element_type.125, (f32[512,1,4,128]{0,3,2,1:T(8,128)S(1)}, f32[1536,1,4,128]{3,0,2,1:T(8,128)}, f32[1536,1,4,128]{3,0,2,1:T(8,128)}) %tuple.329, (s32[]{:T(128)}, ...), branch_computations={%region_26.27_spmd, %region_27.28_spmd} | conditional | flops 1354236928 | bytes 95590664 | solution.py:155
  298.0 27.5 %while.181 = (s32[]{:T(128)}, f32[512,1,4,128]{0,3,2,1:T(8,128)S(1)}, f32[1536,1,4,128]{3,0,2,1:T(8,128)}, f32[1536,1,4,128]{3,0,2,1:T(8,128)}, s32[]{:T(128)}, ...) while((s32[]{:T(128)}, ...), condition=%wide.region_28.30_spmd.clone, body=%wide.region_25.29_spmd.clone.sunk | while | flops 1354236928 | bytes 95591000 | solution.py:158
  299.4 12.8 %conditional.9 = ((f32[512,1,4,128]{0,3,2,1:T(8,128)S(1)}, f32[1536,1,4,128]{3,0,2,1:T(8,128)}, f32[1536,1,4,128]{3,0,2,1:T(8,128)})) conditional(s32[]{:T(128)} %convert_element_type.125, (f32[512,1,4,128]{0,3,2,1:T(8,128)S(1)}, f32[1536,1,4,128]{3,0,2,1:T(8,128)}, f32[1536,1,4,128]{3,0,2,1:T(8,128)}) %tuple.329, (s32[]{:T(128)}, ...), branch_computations={%region_26.27_spmd, %region_27.28_spmd} | conditional | flops 1354236928 | bytes 95590664 | solution.py:155
  312.8 12.8 %conditional.9 = ((f32[512,1,4,128]{0,3,2,1:T(8,128)S(1)}, f32[1536,1,4,128]{3,0,2,1:T(8,128)}, f32[1536,1,4,128]{3,0,2,1:T(8,128)})) conditional(s32[]{:T(128)} %convert_element_type.125, (f32[512,1,4,128]{0,3,2,1:T(8,128)S(1)}, f32[1536,1,4,128]{3,0,2,1:T(8,128)}, f32[1536,1,4,128]{3,0,2,1:T(8,128)}) %tuple.329, (s32[]{:T(128)}, ...), branch_computations={%region_26.27_spmd, %region_27.28_spmd} | conditional | flops 1354236928 | bytes 95590664 | solution.py:155
  339.5 17.3 %all-to-all-done.8 = bf16[192,8,4,128]{3,2,0,1:T(4,128)(2,1)S(1)} async-done(((bf16[192,8,4,128]{3,2,0,1:T(4,128)(2,1)}), bf16[192,8,4,128]{3,2,0,1:T(4,128)(2,1)S(1)}, u32[]{:S(2)}, u32[]{:S(2)}) %all-to-all-start.8) | async-done | bytes 1572896 | tf_op jit(solution)/shard_map/all_to_all | solution.py:244
  364.7 17.4 %all-to-all-done.9 = bf16[192,8,4,128]{3,0,2,1:T(8,128)(2,1)} async-done(((bf16[192,8,4,128]{3,0,2,1:T(8,128)(2,1)}), bf16[192,8,4,128]{3,0,2,1:T(8,128)(2,1)}, u32[]{:S(2)}, u32[]{:S(2)}) %all-to-all-start.9) | async-done | bytes 1572896 | tf_op jit(solution)/shard_map/all_to_all | solution.py:245
  395.0 12.5 %all-to-all-done.10 = bf16[192,8,4,128]{3,0,2,1:T(8,128)(2,1)} async-done(((bf16[192,8,4,128]{3,0,2,1:T(8,128)(2,1)}), bf16[192,8,4,128]{3,0,2,1:T(8,128)(2,1)}, u32[]{:S(2)}, u32[]{:S(2)}) %all-to-all-start.10) | async-done | bytes 1572896 | tf_op jit(solution)/shard_map/all_to_all | solution.py:252
  (327 shorter events, 263.8 us)
Async XLA Ops:
  0.6 40.4 %copy-start = (bf16[128,1,1,4096]{3,0,2,1:T(8,128)(2,1)S(1)}, bf16[128,1,1,4096]{3,0,2,1:T(8,128)(2,1)}, u32[]{:S(2)}) copy-start(bf16[128,1,1,4096]{3,0,2,1:T(8,128)(2,1)} %param.29) | copy-start | bytes 3145732
  0.6 5.7 %copy-start.6 = (bf16[128,1,1,1024]{3,0,2,1:T(8,128)(2,1)S(1)}, bf16[128,1,1,1024]{3,0,2,1:T(8,128)(2,1)}, u32[]{:S(2)}) copy-start(bf16[128,1,1,1024]{3,0,2,1:T(8,128)(2,1)} %param.31) | copy-start | bytes 786436
  8.6 14.4 %all-to-all-start.2 = ((bf16[48,4,1024]{2,0,1:T(8,128)(2,1)}), bf16[48,4,1024]{2,0,1:T(8,128)(2,1)S(1)}, u32[]{:S(2)}, u32[]{:S(2)}) async-start(bf16[48,4,1024]{2,0,1:T(8,128)(2,1)} %copy.149), calls=%async_computation.2 | async-start | bytes 786432 | tf_op jit(solution)/shard_map/all_to_all | solution.py:205
  23.0 14.3 %all-to-all-start.6 = ((bf16[48,4,1024]{2,0,1:T(8,128)(2,1)}), bf16[48,4,1024]{2,0,1:T(8,128)(2,1)S(1)}, u32[]{:S(2)}, u32[]{:S(2)}) async-start(bf16[48,4,1024]{2,0,1:T(8,128)(2,1)} %copy.158), calls=%async_computation.6 | async-start | bytes 786432 | tf_op jit(solution)/shard_map/all_to_all | solution.py:206
  37.3 12.1 %all-to-all-start.3 = ((bf16[192,1,8,128]{3,0,1,2:T(8,128)(2,1)}), bf16[192,1,8,128]{3,0,1,2:T(8,128)(2,1)S(1)}, u32[]{:S(2)}, u32[]{:S(2)}) async-start(bf16[192,1,8,128]{3,0,1,2:T(8,128)(2,1)} %copy.151), calls=%async_computation.3 | async-start | bytes 786432 | tf_op jit(solution)/shard_map/all_to_all | solution.py:232
  46.4 6.4 %copy-start.12 = (bf16[192,4096]{1,0:T(8,128)(2,1)S(1)}, bf16[192,4096]{1,0:T(8,128)(2,1)}, u32[]{:S(2)}) copy-start(bf16[192,4096]{1,0:T(8,128)(2,1)} %gather_fusion) | copy-start | bytes 4718596
  49.4 11.7 %all-to-all-start.7 = ((bf16[192,1,8,128]{3,0,1,2:T(8,128)(2,1)}), bf16[192,1,8,128]{3,0,1,2:T(8,128)(2,1)S(1)}, u32[]{:S(2)}, u32[]{:S(2)}) async-start(bf16[192,1,8,128]{3,0,1,2:T(8,128)(2,1)} %copy.160), calls=%async_computation.7 | async-start | bytes 786432 | tf_op jit(solution)/shard_map/all_to_all | solution.py:233
  61.1 41.1 %all-to-all-start = ((bf16[48,4,4096]{2,0,1:T(8,128)(2,1)}), bf16[48,4,4096]{2,0,1:T(8,128)(2,1)S(1)}, u32[]{:S(2)}, u32[]{:S(2)}) async-start(bf16[48,4,4096]{2,0,1:T(8,128)(2,1)} %copy.145), calls=%async_computation | async-start | bytes 3145728 | tf_op jit(solution)/shard_map/all_to_all | solution.py:204
  103.3 40.3 %all-to-all-start.4 = ((bf16[48,4,4096]{2,0,1:T(8,128)(2,1)}), bf16[48,4,4096]{2,0,1:T(8,128)(2,1)S(1)}, u32[]{:S(2)}, u32[]{:S(2)}) async-start(bf16[48,4,4096]{2,0,1:T(8,128)(2,1)} %copy.154), calls=%async_computation.4 | async-start | bytes 3145728 | tf_op jit(solution)/shard_map/all_to_all | solution.py:207
  117.1 31.5 %copy-start.16 = (s32[192]{0:T(256)S(1)}, s32[192]{0:T(256)}, u32[]{:S(2)}) copy-start(s32[192]{0:T(256)} %param.33) | copy-start | bytes 2308
  117.2 31.5 %copy-start.17 = (s32[192]{0:T(256)S(1)}, s32[192]{0:T(256)}, u32[]{:S(2)}) copy-start(s32[192]{0:T(256)} %param.34) | copy-start | bytes 2308
  117.2 31.5 %copy-start.15 = (s32[192]{0:T(256)S(1)}, s32[192]{0:T(256)}, u32[]{:S(2)}) copy-start(s32[192]{0:T(256)} %param.35) | copy-start | bytes 2308
  144.7 24.9 %all-to-all-start.1 = ((bf16[192,1,32,128]{3,0,1,2:T(8,128)(2,1)}), bf16[192,1,32,128]{3,0,1,2:T(8,128)(2,1)S(1)}, u32[]{:S(2)}, u32[]{:S(2)}) async-start(bf16[192,1,32,128]{3,0,1,2:T(8,128)(2,1)} %copy.147), calls=%async_computation.1 | async-start | bytes 3145728 | tf_op jit(solution)/shard_map/all_to_all | solution.py:230
  170.8 40.1 %all-to-all-start.5 = ((bf16[192,1,32,128]{3,0,1,2:T(8,128)(2,1)}), bf16[192,1,32,128]{3,0,1,2:T(8,128)(2,1)S(1)}, u32[]{:S(2)}, u32[]{:S(2)}) async-start(bf16[192,1,32,128]{3,0,1,2:T(8,128)(2,1)} %copy.156), calls=%async_computation.5 | async-start | bytes 3145728 | tf_op jit(solution)/shard_map/all_to_all | solution.py:231
  264.7 3.8 copy-start.3
  264.7 4.7 %copy-start.7 = (f32[1536,1,4,128]{3,0,2,1:T(8,128)S(1)}, f32[1536,1,4,128]{3,0,2,1:T(8,128)}, u32[]{:S(2)}) copy-start(f32[1536,1,4,128]{3,0,2,1:T(8,128)} %get-tuple-element.1776) | copy-start | bytes 9437188 | tf_op jit(solution)/shard_map/while/body/eval_jaxpr/while/body/cond
  283.5 3.8 copy-start.3
  283.5 4.7 %copy-start.7 = (f32[1536,1,4,128]{3,0,2,1:T(8,128)S(1)}, f32[1536,1,4,128]{3,0,2,1:T(8,128)}, u32[]{:S(2)}) copy-start(f32[1536,1,4,128]{3,0,2,1:T(8,128)} %get-tuple-element.1776) | copy-start | bytes 9437188 | tf_op jit(solution)/shard_map/while/body/eval_jaxpr/while/body/cond
  302.4 4.7 %copy-start.7 = (f32[1536,1,4,128]{3,0,2,1:T(8,128)S(1)}, f32[1536,1,4,128]{3,0,2,1:T(8,128)}, u32[]{:S(2)}) copy-start(f32[1536,1,4,128]{3,0,2,1:T(8,128)} %get-tuple-element.1776) | copy-start | bytes 9437188 | tf_op jit(solution)/shard_map/while/body/eval_jaxpr/while/body/cond
  315.8 4.7 %copy-start.7 = (f32[1536,1,4,128]{3,0,2,1:T(8,128)S(1)}, f32[1536,1,4,128]{3,0,2,1:T(8,128)}, u32[]{:S(2)}) copy-start(f32[1536,1,4,128]{3,0,2,1:T(8,128)} %get-tuple-element.1776) | copy-start | bytes 9437188 | tf_op jit(solution)/shard_map/while/body/eval_jaxpr/while/body/cond
  331.6 25.2 %all-to-all-start.8 = ((bf16[192,8,4,128]{3,2,0,1:T(4,128)(2,1)}), bf16[192,8,4,128]{3,2,0,1:T(4,128)(2,1)S(1)}, u32[]{:S(2)}, u32[]{:S(2)}) async-start(bf16[192,8,4,128]{3,2,0,1:T(4,128)(2,1)} %copy.169), calls=%async_computation.8 | async-start | bytes 3145728 | tf_op jit(solution)/shard_map/all_to_all | solution.py:244
  356.7 25.4 %all-to-all-start.9 = ((bf16[192,8,4,128]{3,0,2,1:T(8,128)(2,1)}), bf16[192,8,4,128]{3,0,2,1:T(8,128)(2,1)}, u32[]{:S(2)}, u32[]{:S(2)}) async-start(bf16[192,8,4,128]{3,0,2,1:T(8,128)(2,1)} %copy.171), calls=%async_computation.9 | async-start | bytes 3145728 | tf_op jit(solution)/shard_map/all_to_all | solution.py:245
  382.1 25.3 %all-to-all-start.10 = ((bf16[192,8,4,128]{3,0,2,1:T(8,128)(2,1)}), bf16[192,8,4,128]{3,0,2,1:T(8,128)(2,1)}, u32[]{:S(2)}, u32[]{:S(2)}) async-start(bf16[192,8,4,128]{3,0,2,1:T(8,128)(2,1)} %copy.173), calls=%async_computation.10 | async-start | bytes 3145728 | tf_op jit(solution)/shard_map/all_to_all | solution.py:252
  393.8 16.6 %copy-start.1 = (bf16[128,1,1,4096]{3,0,2,1:T(8,128)(2,1)S(1)}, bf16[128,1,1,4096]{3,0,2,1:T(8,128)(2,1)}, u32[]{:S(2)}) copy-start(bf16[128,1,1,4096]{3,0,2,1:T(8,128)(2,1)} %param.29) | copy-start | bytes 3145732
  (20 other events, 52.9 us)
where the time goes:
time: 413 us; the launch traced here: 410 us
  waiting for transfers between devices  125 us (30%)
  local copies, waits for them, and re-layouts  121 us (29%)
  starting transfers between devices  50 us (12%)
  matrix products  46.3 us (11%)
  loops' own time  37.3 us (9%)
  other arithmetic  30 us (7%)
    all_to_all x1, waiting for transfers between devices, on_device(): lax.all_to_all(pack_rows(q_src), 'grp', split_axis=1, concat_axis=1, tile...  28.1 us
    all_to_all x1, waiting for transfers between devices, on_device(): lax.all_to_all(pack_rows(grad_src), 'grp', split_axis=1, concat_axis=1, t...  23.2 us
    all_to_all x1, waiting for transfers between devices, on_device(): lax.all_to_all(k_low.reshape(row_count, sp_count, q_local, head_dim), 'sp...  17.4 us
    all_to_all x1, waiting for transfers between devices, on_device(): lax.all_to_all(q_low, 'sp', split_axis=1, concat_axis=2, tiled=True)  17.3 us
    dot_general x4, matrix products, update(): jnp.einsum('qjih,kjh->jiqk', g_block, v_block, preferred_element_type=jnp...  15.2 us
    dynamic_slice x24, local copies, waits for them, and re-layouts, cut_block(): return lax.dynamic_slice_in_dim(array, index * span_len, span_len, 0)  14.4 us
    dot_general x8, matrix products, pair_logits(): jnp.einsum('qjih,kjh->jiqk', q_block, k_block, preferred_element_type=jnp...  14.2 us
    cond x44, local copies, waits for them, and re-layouts  13.9 us
  transfers between devices with their start and end apart: 11, of which 10 were waited for; matrix products, arithmetic and copies ran while one was open for 20% of the time, Pallas kernels for 0%

commit v1 on v0

--- a/solution.py
+++ b/solution.py
@@ -3,6 +3,8 @@
 import jax
 import jax.numpy as jnp
 from jax import lax
+from jax.experimental import pallas as pl
+from jax.experimental.pallas import tpu as pltpu
 from jax.sharding import PartitionSpec as P
 
 HEADS = 32
@@ -164,7 +166,7 @@
     return (grad_q * factor, grad_k * factor, grad_v)
 
 
-def on_device(q_src, k_src, v_src, grad_src, doc_lengths, doc_groups, doc_offsets):
+def on_device_wide(q_src, k_src, v_src, grad_src, doc_lengths, doc_groups, doc_offsets):
     grp_count = lax.axis_size("grp")
     sp_count = lax.axis_size("sp")
     unit_count = q_src.shape[0]
@@ -265,6 +267,340 @@
     return (dq_out, dk_out, dv_out)
 
 
+MESH = pl.DeviceIdType.MESH
+STEP = 16
+F32 = jnp.float32
+BF16 = jnp.bfloat16
+
+
+def dot_nt(left, right):
+    return lax.dot_general(left, right, (((1,), (1,)), ((), ())), preferred_element_type=F32)
+
+
+def dot_nn(left, right):
+    return lax.dot_general(left, right, (((1,), (0,)), ((), ())), preferred_element_type=F32)
+
+
+def fused_kernel(
+    n_grp,
+    n_sp,
+    tiles,
+    q_ref,
+    k_ref,
+    v_ref,
+    g_ref,
+    hot_ref,
+    first_ref,
+    dq_ref,
+    dk_ref,
+    dv_ref,
+    send,
+    recv,
+    home_q,
+    home_kv,
+    back_q,
+    back_kv,
+    bias,
+    k_turned,
+    dk_acc,
+    dv_acc,
+    send_sem,
+    recv_sem,
+    own_sem,
+    hq_send,
+    hq_recv,
+    hkv_send,
+    hkv_recv,
+    hown_sem,
+):
+    my_grp = lax.axis_index("grp")
+    my_sp = lax.axis_index("sp")
+    peers = n_grp * n_sp
+    me = my_grp * n_sp + my_sp
+    q_wide = q_ref.shape[1] // n_sp
+    kv_wide = k_ref.shape[1] // n_sp
+    heads = q_wide // kv_wide
+    tile_tok = peers * STEP
+    factor = HEAD_DIM ** (-0.5)
+
+    barrier = pltpu.get_barrier_semaphore()
+
+    @pl.loop(1, peers)
+    def _(hop):
+        there = {
+            "grp": lax.rem(my_grp + hop // n_sp, n_grp),
+            "sp": lax.rem(my_sp + lax.rem(hop, n_sp), n_sp),
+        }
+        pl.semaphore_signal(barrier, inc=1, device_id=there, device_id_type=MESH)
+
+    def pack(tile):
+        hot = hot_ref[tile]
+        for to in range(n_sp):
+            at = 0
+            for ref, wide in ((q_ref, q_wide), (k_ref, kv_wide), (v_ref, kv_wide), (g_ref, q_wide)):
+                part = dot_nn(hot, ref[:, to * wide : (to + 1) * wide]).astype(BF16)
+                part = part.reshape(n_grp, STEP, wide)
+                for grp in range(n_grp):
+                    send[tile, grp * n_sp + to, :, at : at + wide] = part[grp]
+                at += wide
+
+    def scatter(tile):
+        @pl.loop(1, peers)
+        def _(hop):
+            turned = lax.rem(hop + 2 * n_sp, peers)
+            to_grp = lax.rem(my_grp + turned // n_sp, n_grp)
+            to_sp = lax.rem(my_sp + lax.rem(turned, n_sp), n_sp)
+
+            @pl.when(turned != 0)
+            def _():
+                pltpu.make_async_remote_copy(
+                    src_ref=send.at[tile, to_grp * n_sp + to_sp],
+                    dst_ref=recv.at[tile, me],
+                    send_sem=send_sem.at[tile],
+                    recv_sem=recv_sem.at[tile],
+                    device_id={"grp": to_grp, "sp": to_sp},
+                    device_id_type=MESH,
+                ).start()
+
+        turned_grp = lax.rem(my_grp + 2, n_grp)
+        pltpu.make_async_remote_copy(
+            src_ref=send.at[tile, turned_grp * n_sp + my_sp],
+            dst_ref=recv.at[tile, me],
+            send_sem=send_sem.at[tile],
+            recv_sem=recv_sem.at[tile],
+            device_id={"grp": turned_grp, "sp": my_sp},
+            device_id_type=MESH,
+        ).start()
+        own = pltpu.make_async_copy(send.at[tile, me], recv.at[tile, me], own_sem.at[tile])
+        own.start()
+        return own
+
+    own_copies = []
+    pack(0)
+    pl.semaphore_wait(barrier, peers - 1)
+    for tile in range(tiles):
+        if tile > 0:
+            pack(tile)
+        own_copies.append(scatter(tile))
+
+    dk_acc[...] = jnp.zeros_like(dk_acc)
+    dv_acc[...] = jnp.zeros_like(dv_acc)
+
+    def go_home(here, back, sends, recvs, own_sem_ref):
+        @pl.loop(1, n_sp)
+        def _(hop):
+            to_sp = lax.rem(my_sp + hop, n_sp)
+            pltpu.make_async_remote_copy(
+                src_ref=here.at[:, to_sp],
+                dst_ref=back.at[:, my_sp],
+                send_sem=sends,
+                recv_sem=recvs,
+                device_id={"grp": my_grp, "sp": to_sp},
+                device_id_type=MESH,
+            ).start()
+
+        own = pltpu.make_async_copy(here.at[:, my_sp], back.at[:, my_sp], own_sem_ref)
+        own.start()
+        return own
+
+    def kv_home(tile):
+        shape = (n_grp, n_sp, STEP, HEAD_DIM)
+        home_kv[tile, :, :, :, :HEAD_DIM] = (dk_acc[tile] * factor).astype(BF16).reshape(shape)
+        home_kv[tile, :, :, :, HEAD_DIM:] = dv_acc[tile].astype(BF16).reshape(shape)
+        return go_home(
+            home_kv.at[tile], back_kv.at[tile], hkv_send.at[tile], hkv_recv.at[tile], hown_sem.at[1, tile]
+        )
+
+    def rows_of(tile, at):
+        return recv[tile, :, :, at : at + HEAD_DIM].reshape(tile_tok, HEAD_DIM)
+
+    k_at = q_wide
+    v_at = q_wide + kv_wide
+    g_at = q_wide + 2 * kv_wide
+    home_own = []
+    for tile in range(tiles):
+        own_copies[tile].wait()
+        pltpu.make_async_copy(
+            recv.at[tile, pl.ds(0, peers - 1)], recv.at[tile, pl.ds(0, peers - 1)], recv_sem.at[tile]
+        ).wait()
+        key_tiles = [tile] if tile == 0 else [tile, tile - 1]
+        lane = lax.broadcasted_iota(jnp.int32, (1, tile_tok), 1)
+        row = lax.broadcasted_iota(jnp.int32, (tile_tok, 1), 0)
+        q_pos = (tile * STEP + lax.rem(lane, STEP)) * peers + lane // STEP
+        q_first = first_ref[tile : tile + 1, :]
+        for n, key_tile in enumerate(key_tiles):
+            k_pos = (key_tile * STEP + lax.rem(row, STEP)) * peers + row // STEP
+            allowed = (k_pos <= q_pos) & (k_pos >= q_first)
+            bias[n] = jnp.where(allowed, 0.0, NEG_FILL)
+            k_turned[n] = rows_of(key_tile, k_at).astype(F32).T.astype(BF16)
+
+        @pl.loop(0, heads)
+        def _(head):
+            at = pl.multiple_of(head * HEAD_DIM, HEAD_DIM)
+            q_head = recv[tile, :, :, pl.ds(at, HEAD_DIM)].reshape(tile_tok, HEAD_DIM)
+            g_head = recv[tile, :, :, pl.ds(at + g_at, HEAD_DIM)].reshape(tile_tok, HEAD_DIM)
+            logits = [
+                dot_nt(rows_of(key_tile, k_at), q_head) * factor + bias[n]
+                for n, key_tile in enumerate(key_tiles)
+            ]
+            high = jnp.max(logits[0], axis=0, keepdims=True)
+            for part in logits[1:]:
+                high = jnp.maximum(high, jnp.max(part, axis=0, keepdims=True))
+            probs = [jnp.exp(part - high) for part in logits]
+            mass = sum(jnp.sum(part, axis=0, keepdims=True) for part in probs)
+            scale = 1.0 / mass
+            probs = [part * scale for part in probs]
+            d_probs = [dot_nt(rows_of(key_tile, v_at), g_head) for key_tile in key_tiles]
+            delta = sum(
+                jnp.sum(part * d_part, axis=0, keepdims=True) for part, d_part in zip(probs, d_probs)
+            )
+            dq_turned = jnp.zeros((HEAD_DIM, tile_tok), F32)
+            for n, key_tile in enumerate(key_tiles):
+                d_logits = (probs[n] * (d_probs[n] - delta)).astype(BF16)
+                dv_acc[key_tile] += dot_nn(probs[n].astype(BF16), g_head)
+                dk_acc[key_tile] += dot_nn(d_logits, q_head)
+                dq_turned += dot_nn(k_turned[n], d_logits)
+            dq_head = (dq_turned * factor).T.astype(BF16)
+            home_q[tile, :, :, :, pl.ds(at, HEAD_DIM)] = dq_head.reshape(n_grp, n_sp, STEP, HEAD_DIM)
+
+        home_own.append(
+            go_home(home_q.at[tile], back_q.at[tile], hq_send.at[tile], hq_recv.at[tile], hown_sem.at[0, tile])
+        )
+        if tile > 0:
+            home_own.append(kv_home(tile - 1))
+    home_own.append(kv_home(tiles - 1))
+
+    out_rows = n_grp * STEP
+    to_row = lax.broadcasted_iota(jnp.int32, (out_rows, out_rows), 0)
+    from_row = lax.broadcasted_iota(jnp.int32, (out_rows, out_rows), 1)
+    weave = (to_row == lax.rem(from_row, STEP) * n_grp + from_row // STEP).astype(BF16)
+    for own in home_own:
+        own.wait()
+    for tile in range(tiles):
+        rows = pl.ds(tile * out_rows, out_rows)
+        arrived_q = back_q.at[tile, :, pl.ds(0, n_sp - 1)]
+        pltpu.make_async_copy(arrived_q, arrived_q, hq_recv.at[tile]).wait()
+        for sp in range(n_sp):
+            part = back_q[tile, :, sp].reshape(out_rows, q_wide)
+            dq_ref[rows, sp * q_wide : (sp + 1) * q_wide] = dot_nn(weave, part).astype(BF16)
+    for tile in range(tiles):
+        rows = pl.ds(tile * out_rows, out_rows)
+        arrived_kv = back_kv.at[tile, :, pl.ds(0, n_sp - 1)]
+        pltpu.make_async_copy(arrived_kv, arrived_kv, hkv_recv.at[tile]).wait()
+        for sp in range(n_sp):
+            part = back_kv[tile, :, sp].reshape(out_rows, 2 * kv_wide)
+            both = dot_nn(weave, part).astype(BF16)
+            dk_ref[rows, sp * kv_wide : (sp + 1) * kv_wide] = both[:, :kv_wide]
+            dv_ref[rows, sp * kv_wide : (sp + 1) * kv_wide] = both[:, kv_wide:]
+    for tile in range(tiles):
+        sent = send.at[tile, pl.ds(0, peers - 1)]
+        pltpu.make_async_copy(sent, sent, send_sem.at[tile]).wait()
+        sent_q = home_q.at[tile, :, pl.ds(0, n_sp - 1)]
+        pltpu.make_async_copy(sent_q, sent_q, hq_send.at[tile]).wait()
+        sent_kv = home_kv.at[tile, :, pl.ds(0, n_sp - 1)]
+        pltpu.make_async_copy(sent_kv, sent_kv, hkv_send.at[tile]).wait()
+
+
+def on_device_fused(q_src, k_src, v_src, grad_src, doc_lengths, doc_groups, doc_offsets):
+    n_grp = lax.axis_size("grp")
+    n_sp = lax.axis_size("sp")
+    units = q_src.shape[0]
+    slots = doc_lengths.shape[0]
+    cap = slots // n_grp
+    tiles = cap // STEP
+    peers = n_grp * n_sp
+    q_all = q_src.shape[-1]
+    kv_all = k_src.shape[-1]
+    q_wide = q_all // n_sp
+    kv_wide = kv_all // n_sp
+    row_wide = 2 * (q_wide + kv_wide)
+    tile_tok = peers * STEP
+
+    starts = jnp.cumsum(doc_lengths) - doc_lengths
+    unit_ids = jnp.arange(units, dtype=jnp.int32)
+    inside = (unit_ids[:, None] >= starts[None, :]) & (
+        unit_ids[:, None] < (starts + doc_lengths)[None, :]
+    )
+    slot_start = doc_groups * cap + doc_offsets - starts
+    slot_of = jnp.sum(jnp.where(inside, slot_start[None, :], 0), axis=1) + unit_ids
+    slot_ids = (
+        jnp.arange(tiles, dtype=jnp.int32)[:, None, None] * STEP
+        + jnp.arange(n_grp, dtype=jnp.int32)[None, :, None] * cap
+        + jnp.arange(STEP, dtype=jnp.int32)[None, None, :]
+    ).reshape(tiles, n_grp * STEP)
+    hot = (slot_ids[:, :, None] == slot_of[None, None, :]).astype(BF16)
+
+    my_group = lax.axis_index("grp")
+    lane = jnp.arange(tile_tok, dtype=jnp.int32)
+    block = jnp.arange(tiles, dtype=jnp.int32)[:, None] * STEP + (lane % STEP)[None, :]
+    member = (
+        (doc_groups == my_group)
+        & (doc_lengths > 0)
+        & (doc_offsets <= block[:, :, None])
+        & (block[:, :, None] < doc_offsets + doc_lengths)
+    )
+    first_unit = jnp.sum(jnp.where(member, doc_offsets * peers, 0), axis=2)
+    occupied = jnp.any(member, axis=2)
+    first = jnp.where(occupied, first_unit, block * peers + (lane // STEP)[None, :])
+
+    rows = cap * n_grp
+    vmem = pl.BlockSpec(memory_space=pltpu.VMEM)
+    dma = pltpu.SemaphoreType.DMA
+    dq, dk, dv = pl.pallas_call(
+        lambda *refs: fused_kernel(n_grp, n_sp, tiles, *refs),
+        out_shape=(
+            jax.ShapeDtypeStruct((rows, q_all), BF16),
+            jax.ShapeDtypeStruct((rows, kv_all), BF16),
+            jax.ShapeDtypeStruct((rows, kv_all), BF16),
+        ),
+        in_specs=[vmem] * 6,
+        out_specs=(vmem,) * 3,
+        scratch_shapes=[
+            pltpu.VMEM((tiles, peers, STEP, row_wide), BF16),
+            pltpu.VMEM((tiles, peers, STEP, row_wide), BF16),
+            pltpu.VMEM((tiles, n_grp, n_sp, STEP, q_wide), BF16),
+            pltpu.VMEM((tiles, n_grp, n_sp, STEP, 2 * kv_wide), BF16),
+            pltpu.VMEM((tiles, n_grp, n_sp, STEP, q_wide), BF16),
+            pltpu.VMEM((tiles, n_grp, n_sp, STEP, 2 * kv_wide), BF16),
+            pltpu.VMEM((2, tile_tok, tile_tok), F32),
+            pltpu.VMEM((2, HEAD_DIM, tile_tok), BF16),
+            pltpu.VMEM((tiles, tile_tok, HEAD_DIM), F32),
+            pltpu.VMEM((tiles, tile_tok, HEAD_DIM), F32),
+            dma((tiles,)),
+            dma((tiles,)),
+            dma((tiles,)),
+            dma((tiles,)),
+            dma((tiles,)),
+            dma((tiles,)),
+            dma((tiles,)),
+            dma((2, tiles)),
+        ],
+        compiler_params=pltpu.CompilerParams(
+            collective_id=0, has_side_effects=True, vmem_limit_bytes=56 * 1024 * 1024
+        ),
+    )(
+        q_src.reshape(units, q_all),
+        k_src.reshape(units, kv_all),
+        v_src.reshape(units, kv_all),
+        grad_src.reshape(units, q_all),
+        hot,
+        first,
+    )
+    return (
+        dq.reshape(1, rows, 1, q_all),
+        dk.reshape(1, rows, 1, kv_all),
+        dv.reshape(1, rows, 1, kv_all),
+    )
+
+
+def on_device(q_src, k_src, v_src, grad_src, doc_lengths, doc_groups, doc_offsets):
+    n_grp = lax.axis_size("grp")
+    cap = doc_lengths.shape[0] // n_grp
+    fits = lax.axis_size("sp") == KV_HEADS and cap % STEP == 0
+    chosen = on_device_fused if fits else on_device_wide
+    return chosen(q_src, k_src, v_src, grad_src, doc_lengths, doc_groups, doc_offsets)
+
+
 def solution(mesh):
     placed = (
         P(None, "grp", "sp", None),

time: 413 us -> 130 us (0.31)
  the two profiles are of different devices: /device:TPU:24 before, /device:TPU:17 now
where the time goes in v1:
time: 130 us; the launch traced here: 128 us
  Pallas kernels  116 us (89%)
  other arithmetic  5.74 us (4%)
  local copies, waits for them, and re-layouts  5.39 us (4%)
    pallas_call x1, Pallas kernels, on_device_fused(): pl.pallas_call(lambda *refs: fused_kernel(n_grp, n_sp, tiles, *refs), out...  116 us
    unnamed x7, local copies, waits for them, and re-layouts  4.27 us

profile of v1, /device:TPU:17, one launch (start us, length us, event | category | flops | bytes accessed | tf_op | source)
XLA Modules:
  0.0 128.2 jit_solution(9758140331438422375)
XLA Ops:
  0.6 0.7 compare_and_fusion.1
  1.3 0.7 pad_bitcast_fusion
  2.0 0.3 reduce-window.9
  2.3 0.1 slice.8
  2.5 0.1 slice_reduce_fusion
  2.6 0.1 add_bitcast_fusion
  2.6 0.1 broadcast_add_fusion.2
  2.7 0.1 add.121
  2.8 0.1 add.118
  2.9 0.1 add.119
  3.0 0.7 add_subtract_fusion
  3.7 0.2 select_reduce_fusion.1
  3.9 0.1 broadcast_add_fusion
  3.9 1.0 fusion
  5.0 1.2 select_reduce_fusion
  6.1 0.7 add_select_fusion.refs_5_
  6.8 0.7 compare_convert_fusion.refs_4_
  7.5 116.4 %shard_map.94 = (bf16[192,4096]{1,0:T(8,128)(2,1)}, bf16[192,1024]{1,0:T(8,128)(2,1)}, bf16[192,1024]{1,0:T(8,128)(2,1)}) custom-call(bf16[128,4096]{1,0:T(8,128)(2,1)} %bitcast.12, bf16[128,1024]{1,0:T(8,128)(2,1)} %bitcast.16, bf16[128,1024]{1,0:T(8,128)(2,1)} %bitcast.17, bf16[128,4096]{1,0:T(8,128)(2,1)} %bitcast.13, ...), custom_call_target="tpu_custom_call" | custom-call | tf_op jit(solution)/shard_map/pallas_call | solution.py:549
  123.9 0.0 copy-start.1
  123.9 0.0 copy-start
  123.9 2.8 %copy.13 = bf16[1,192,1,4096]{3,1,2,0:T(8,128)(2,1)} copy(bf16[1,192,1,4096]{3,1,2,0:T(8,128)(2,1)} %bitcast.11) | data formatting | bytes 3145728
  126.7 0.0 copy-done.1
  126.7 0.7 copy.14
  127.5 0.7 copy.15
  (8 shorter events, 0.1 us)
Async XLA Ops:
  123.9 2.8 %copy-start.1 = (bf16[192,1024]{1,0:T(8,128)(2,1)S(1)}, bf16[192,1024]{1,0:T(8,128)(2,1)}, u32[]{:S(2)}) copy-start(bf16[192,1024]{1,0:T(8,128)(2,1)} %get-tuple-element.7) | copy-start | bytes 1179652
  123.9 3.5 %copy-start = (bf16[192,1024]{1,0:T(8,128)(2,1)S(1)}, bf16[192,1024]{1,0:T(8,128)(2,1)}, u32[]{:S(2)}) copy-start(bf16[192,1024]{1,0:T(8,128)(2,1)} %get-tuple-element.8) | copy-start | bytes 1179652

commit v2 on v0

--- a/solution.py
+++ b/solution.py
@@ -3,6 +3,8 @@
 import jax
 import jax.numpy as jnp
 from jax import lax
+from jax.experimental import pallas as pl
+from jax.experimental.pallas import tpu as pltpu
 from jax.sharding import PartitionSpec as P
 
 HEADS = 32
@@ -164,7 +166,7 @@
     return (grad_q * factor, grad_k * factor, grad_v)
 
 
-def on_device(q_src, k_src, v_src, grad_src, doc_lengths, doc_groups, doc_offsets):
+def on_device_wide(q_src, k_src, v_src, grad_src, doc_lengths, doc_groups, doc_offsets):
     grp_count = lax.axis_size("grp")
     sp_count = lax.axis_size("sp")
     unit_count = q_src.shape[0]
@@ -265,6 +267,436 @@
     return (dq_out, dk_out, dv_out)
 
 
+MESH = pl.DeviceIdType.MESH
+STEP = 16
+MAXDOC = 5
+F32 = jnp.float32
+BF16 = jnp.bfloat16
+
+
+def dot_nt(left, right):
+    return lax.dot_general(left, right, (((1,), (1,)), ((), ())), preferred_element_type=F32)
+
+
+def dot_nn(left, right):
+    return lax.dot_general(left, right, (((1,), (0,)), ((), ())), preferred_element_type=F32)
+
+
+def lane_iota(rows, lanes):
+    return lax.broadcasted_iota(jnp.int32, (rows, lanes), 1)
+
+
+def row_iota(rows, lanes):
+    return lax.broadcasted_iota(jnp.int32, (rows, lanes), 0)
+
+
+def fused_kernel(
+    n_grp,
+    n_sp,
+    tiles,
+    q_ref,
+    k_ref,
+    v_ref,
+    g_ref,
+    len_ref,
+    grp_ref,
+    off_ref,
+    back_q,
+    back_kv,
+    send,
+    recv,
+    home_q,
+    home_kv,
+    bias,
+    halo_bias,
+    halo_kv,
+    k_turned,
+    halo_turned,
+    d_acc,
+    halo_acc,
+    send_sem,
+    recv_sem,
+    own_sem,
+    hq_send,
+    hq_recv,
+    hq_own,
+    hkv_send,
+    hkv_recv,
+    hkv_own,
+):
+    my_grp = lax.axis_index("grp")
+    my_sp = lax.axis_index("sp")
+    peers = n_grp * n_sp
+    me = my_grp * n_sp + my_sp
+    units = q_ref.shape[0]
+    q_wide = q_ref.shape[1] // n_sp
+    heads = q_wide // HEAD_DIM
+    cap = tiles * STEP
+    tile_tok = peers * STEP
+    halo = MAXDOC - 1
+    halo_tok = peers * halo
+    factor = HEAD_DIM ** (-0.5)
+    row_wide = 2 * HEAD_DIM * (heads + 1)
+    last = tiles - 1
+    kv_lanes = pl.ds(0, 2 * HEAD_DIM)
+
+    barrier = pltpu.get_barrier_semaphore()
+
+    @pl.loop(1, peers)
+    def _(hop):
+        there = {
+            "grp": lax.rem(my_grp + hop // n_sp, n_grp),
+            "sp": lax.rem(my_sp + lax.rem(hop, n_sp), n_sp),
+        }
+        pl.semaphore_signal(barrier, inc=1, device_id=there, device_id_type=MESH)
+
+    slots = len_ref.shape[1]
+    which = row_iota(8, slots)
+    tables = jnp.where(
+        which == 0, len_ref[...], jnp.where(which == 1, grp_ref[...], jnp.where(which == 2, off_ref[...], 0))
+    )
+    tables = tables.astype(F32).astype(BF16)
+    down, across = row_iota(slots, slots), lane_iota(slots, slots)
+    columns = dot_nt((down == across).astype(F32).astype(BF16), tables)
+    length, group, offset = columns[:, 0:1], columns[:, 1:2], columns[:, 2:3]
+    start = dot_nt((across < down).astype(F32).astype(BF16), tables)[:, 0:1]
+    unit = lane_iota(1, units).astype(F32)
+    inside = (unit >= start) & (unit < start + length)
+    slot_of = unit + jnp.sum(
+        jnp.where(inside, group * cap + offset - start, 0.0), axis=0, keepdims=True
+    )
+
+    def pack(tile):
+        row = row_iota(n_grp * STEP, 1)
+        slot = (row // STEP) * cap + tile * STEP + lax.rem(row, STEP)
+        hot = (slot.astype(F32) == slot_of).astype(F32).astype(BF16)
+
+        def put(to, at, ref, lane, wide):
+            part = dot_nn(hot, ref[:, lane : lane + wide]).astype(BF16).reshape(n_grp, STEP, wide)
+            for grp in range(n_grp):
+                send[tile, grp * n_sp + to, :, at : at + wide] = part[grp]
+
+        for to in range(n_sp):
+            put(to, 0, k_ref, to * HEAD_DIM, HEAD_DIM)
+            put(to, HEAD_DIM, v_ref, to * HEAD_DIM, HEAD_DIM)
+            for head in range(heads):
+                lane = to * q_wide + head * HEAD_DIM
+                put(to, 2 * HEAD_DIM * (head + 1), q_ref, lane, HEAD_DIM)
+                put(to, 2 * HEAD_DIM * (head + 1) + HEAD_DIM, g_ref, lane, HEAD_DIM)
+
+    def scatter(tile, lane, wide, sem):
+        lanes = pl.ds(lane, wide)
+
+        def push(to_grp, to_sp):
+            pltpu.make_async_remote_copy(
+                src_ref=send.at[tile, to_grp * n_sp + to_sp, :, lanes],
+                dst_ref=recv.at[tile, me, :, lanes],
+                send_sem=send_sem.at[sem],
+                recv_sem=recv_sem.at[sem],
+                device_id={"grp": to_grp, "sp": to_sp},
+                device_id_type=MESH,
+            ).start()
+
+        for turn in [n_grp // 2] + [t for t in range(1, n_grp) if t != n_grp // 2] + [0]:
+
+            @pl.loop(1 if turn == 0 else 0, n_sp)
+            def _(hop):
+                push(lax.rem(my_grp + turn, n_grp), lax.rem(my_sp + hop, n_sp))
+
+    def landed(tile, lane, wide, sem):
+        block = recv.at[tile, pl.ds(0, peers - 1), :, pl.ds(lane, wide)]
+        pltpu.make_async_copy(block, block, recv_sem.at[sem]).wait()
+
+    def own_block(tile):
+        return pltpu.make_async_copy(send.at[tile, me], recv.at[tile, me], own_sem.at[tile])
+
+    pack(0)
+    pl.semaphore_wait(barrier, peers - 1)
+    for tile in range(last):
+        if tile > 0:
+            pack(tile)
+        scatter(tile, 0, row_wide, tile)
+    pack(last)
+    pair = 2 * HEAD_DIM
+    scatter(last, 0, 2 * pair, last)
+    for head in range(1, heads):
+        scatter(last, (head + 1) * pair, pair, last + head)
+    for tile in range(tiles):
+        own_block(tile).start()
+
+    d_acc[...] = jnp.zeros_like(d_acc)
+
+    def go_home(here, back, sends, recvs, own):
+        @pl.loop(1, n_sp)
+        def _(hop):
+            to_sp = lax.rem(my_sp + hop, n_sp)
+            pltpu.make_async_remote_copy(
+                src_ref=here.at[:, to_sp],
+                dst_ref=back.at[:, my_sp],
+                send_sem=sends,
+                recv_sem=recvs,
+                device_id={"grp": my_grp, "sp": to_sp},
+                device_id_type=MESH,
+            ).start()
+
+        pltpu.make_async_copy(here.at[:, my_sp], back.at[:, my_sp], own).start()
+
+    def kv_home(tile):
+        shape = (n_grp, n_sp, STEP, HEAD_DIM)
+        home_kv[tile, :, :, :, :HEAD_DIM] = (
+            (d_acc[tile, :, :HEAD_DIM] * factor).astype(BF16).reshape(shape)
+        )
+        home_kv[tile, :, :, :, HEAD_DIM:] = d_acc[tile, :, HEAD_DIM:].astype(BF16).reshape(shape)
+        go_home(
+            home_kv.at[tile], back_kv.at[tile], hkv_send.at[tile], hkv_recv.at[tile], hkv_own.at[tile]
+        )
+
+    halo_row = row_iota(halo_tok, 1)
+    halo_from = (halo_row // halo) * STEP + STEP - halo + lax.rem(halo_row, halo)
+    cut = (halo_from == lane_iota(1, tile_tok)).astype(F32).astype(BF16)
+    row = row_iota(tile_tok, 1)
+    halo_lane = lane_iota(1, halo_tok)
+    paste = (
+        row == (halo_lane // halo) * STEP + STEP - halo + lax.rem(halo_lane, halo)
+    ).astype(F32)
+
+    for tile in range(tiles):
+        lane = lane_iota(1, tile_tok)
+        q_block = tile * STEP + lax.rem(lane, STEP)
+        q_pos = q_block * peers + lane // STEP
+        place = q_block.astype(F32)
+        member = (
+            (group == my_grp.astype(F32))
+            & (length > 0.0)
+            & (offset <= place)
+            & (place < offset + length)
+        )
+        first = jnp.sum(jnp.where(member, offset * peers, 0.0), axis=0, keepdims=True)
+        occupied = jnp.sum(jnp.where(member, 1.0, 0.0), axis=0, keepdims=True) > 0.0
+        first = jnp.where(occupied, first, q_pos.astype(F32)).astype(jnp.int32)
+        k_pos = (tile * STEP + lax.rem(row, STEP)) * peers + row // STEP
+        bias[...] = jnp.where((k_pos <= q_pos) & (k_pos >= first), 0.0, NEG_FILL)
+        if tile > 0:
+            halo_pos = (tile * STEP - halo + lax.rem(halo_row, halo)) * peers + halo_row // halo
+            halo_bias[...] = jnp.where(halo_pos >= first, 0.0, NEG_FILL)
+            kv_before = recv[tile - 1, :, :, : 2 * HEAD_DIM].reshape(tile_tok, 2 * HEAD_DIM)
+            kv_cut = dot_nn(cut, kv_before)
+            halo_kv[...] = kv_cut.astype(BF16)
+            halo_turned[...] = kv_cut[:, :HEAD_DIM].T.astype(BF16)
+            halo_acc[...] = jnp.zeros_like(halo_acc)
+
+        own_block(tile).wait()
+        landed(tile, 0, 2 * pair if tile == last else row_wide, tile)
+        k_turned[...] = (
+            recv[tile, :, :, :HEAD_DIM].reshape(tile_tok, HEAD_DIM).astype(F32).T.astype(BF16)
+        )
+
+        @pl.loop(0, heads)
+        def _(head):
+            if tile == last:
+
+                @pl.when(head > 0)
+                def _():
+                    landed(last, pair, pair, last + head)
+
+            at = pl.multiple_of(head * HEAD_DIM, HEAD_DIM)
+            q_at = pl.multiple_of((head + 1) * pair, HEAD_DIM)
+            g_at = pl.multiple_of((head + 1) * pair + HEAD_DIM, HEAD_DIM)
+            q_head = recv[tile, :, :, pl.ds(q_at, HEAD_DIM)].reshape(tile_tok, HEAD_DIM)
+            g_head = recv[tile, :, :, pl.ds(g_at, HEAD_DIM)].reshape(tile_tok, HEAD_DIM)
+            keys = [recv[tile, :, :, :HEAD_DIM].reshape(tile_tok, HEAD_DIM)]
+            vals = [recv[tile, :, :, HEAD_DIM : 2 * HEAD_DIM].reshape(tile_tok, HEAD_DIM)]
+            masks = [bias]
+            turned = [k_turned]
+            if tile > 0:
+                keys.append(halo_kv[:, :HEAD_DIM])
+                vals.append(halo_kv[:, HEAD_DIM:])
+                masks.append(halo_bias)
+                turned.append(halo_turned)
+            logits = [dot_nt(key, q_head) * factor + mask[...] for key, mask in zip(keys, masks)]
+            high = jnp.max(logits[0], axis=0, keepdims=True)
+            for part in logits[1:]:
+                high = jnp.maximum(high, jnp.max(part, axis=0, keepdims=True))
+            probs = [jnp.exp(part - high) for part in logits]
+            mass = sum(jnp.sum(part, axis=0, keepdims=True) for part in probs)
+            scale = 1.0 / mass
+            probs = [part * scale for part in probs]
+            d_probs = [dot_nt(val, g_head) for val in vals]
+            delta = sum(
+                jnp.sum(part * d_part, axis=0, keepdims=True) for part, d_part in zip(probs, d_probs)
+            )
+            dq_turned = jnp.zeros((HEAD_DIM, tile_tok), F32)
+            for n in range(len(keys)):
+                d_logits = (probs[n] * (d_probs[n] - delta)).astype(BF16)
+                d_key = dot_nn(d_logits, q_head)
+                d_val = dot_nn(probs[n].astype(BF16), g_head)
+                if n == 0:
+                    d_acc[tile, :, :HEAD_DIM] += d_key
+                    d_acc[tile, :, HEAD_DIM:] += d_val
+                else:
+                    halo_acc[:, :HEAD_DIM] += d_key
+                    halo_acc[:, HEAD_DIM:] += d_val
+                dq_turned += dot_nn(turned[n][...], d_logits)
+            dq_head = (dq_turned * factor).T.astype(BF16)
+            lanes = pl.ds(at, HEAD_DIM)
+            home_q[tile, :, :, :, lanes] = dq_head.reshape(n_grp, n_sp, STEP, HEAD_DIM)
+            if tile == last:
+                go_home(
+                    home_q.at[tile, :, :, :, lanes],
+                    back_q.at[tile, :, :, :, lanes],
+                    hq_send.at[last + head],
+                    hq_recv.at[last + head],
+                    hq_own.at[last + head],
+                )
+
+        if tile < last:
+            go_home(
+                home_q.at[tile], back_q.at[tile], hq_send.at[tile], hq_recv.at[tile], hq_own.at[tile]
+            )
+        if tile > 0:
+            d_acc[tile - 1] += lax.dot_general(
+                paste,
+                halo_acc[...],
+                (((1,), (0,)), ((), ())),
+                precision=lax.Precision.HIGHEST,
+                preferred_element_type=F32,
+            )
+            kv_home(tile - 1)
+    kv_home(last)
+
+    def settle(block, sem):
+        pltpu.make_async_copy(block, block, sem).wait()
+
+    away = pl.ds(0, n_sp - 1)
+    for tile in range(tiles):
+        settle(home_kv.at[tile, :, 0], hkv_own.at[tile])
+        settle(home_kv.at[tile, :, away], hkv_send.at[tile])
+        settle(home_kv.at[tile, :, away], hkv_recv.at[tile])
+    for tile in range(last):
+        settle(home_q.at[tile, :, 0], hq_own.at[tile])
+        settle(home_q.at[tile, :, away], hq_send.at[tile])
+        settle(home_q.at[tile, :, away], hq_recv.at[tile])
+        settle(send.at[tile, pl.ds(0, peers - 1)], send_sem.at[tile])
+    for head in range(heads):
+        settle(home_q.at[last, :, 0, :, :HEAD_DIM], hq_own.at[last + head])
+        settle(home_q.at[last, :, away, :, :HEAD_DIM], hq_send.at[last + head])
+        settle(home_q.at[last, :, away, :, :HEAD_DIM], hq_recv.at[last + head])
+        wide = 2 * pair if head == 0 else pair
+        settle(send.at[last, pl.ds(0, peers - 1), :, :wide], send_sem.at[last + head])
+
+
+def weave_kernel(back_q, back_kv, dq_ref, dk_ref, dv_ref):
+    n_grp, n_sp, step, q_wide = back_q.shape
+    rows = n_grp * step
+    from_row = lane_iota(rows, rows)
+    weave = row_iota(rows, rows) == lax.rem(from_row, step) * n_grp + from_row // step
+    weave = weave.astype(F32).astype(BF16)
+    for sp in range(n_sp):
+        part = dot_nn(weave, back_q[:, sp].reshape(rows, q_wide)).astype(BF16)
+        dq_ref[:, sp * q_wide : (sp + 1) * q_wide] = part
+        both = dot_nn(weave, back_kv[:, sp].reshape(rows, 2 * HEAD_DIM)).astype(BF16)
+        dk_ref[:, sp * HEAD_DIM : (sp + 1) * HEAD_DIM] = both[:, :HEAD_DIM]
+        dv_ref[:, sp * HEAD_DIM : (sp + 1) * HEAD_DIM] = both[:, HEAD_DIM:]
+
+
+def on_device_fused(q_src, k_src, v_src, grad_src, doc_lengths, doc_groups, doc_offsets):
+    n_grp = lax.axis_size("grp")
+    n_sp = lax.axis_size("sp")
+    units = q_src.shape[0]
+    slots = doc_lengths.shape[0]
+    cap = slots // n_grp
+    tiles = cap // STEP
+    peers = n_grp * n_sp
+    q_all = q_src.shape[-1]
+    kv_all = k_src.shape[-1]
+    q_wide = q_all // n_sp
+    heads = q_wide // HEAD_DIM
+    row_wide = 2 * HEAD_DIM * (heads + 1)
+    tile_tok = peers * STEP
+    halo_tok = peers * (MAXDOC - 1)
+    parts = tiles - 1 + heads
+
+    vmem = pl.BlockSpec(memory_space=pltpu.VMEM)
+    hbm = pl.BlockSpec(memory_space=pl.ANY)
+    dma = pltpu.SemaphoreType.DMA
+    back_q, back_kv = pl.pallas_call(
+        lambda *refs: fused_kernel(n_grp, n_sp, tiles, *refs),
+        out_shape=(
+            jax.ShapeDtypeStruct((tiles, n_grp, n_sp, STEP, q_wide), BF16),
+            jax.ShapeDtypeStruct((tiles, n_grp, n_sp, STEP, 2 * HEAD_DIM), BF16),
+        ),
+        in_specs=[vmem] * 7,
+        out_specs=(hbm, hbm),
+        scratch_shapes=[
+            pltpu.VMEM((tiles, peers, STEP, row_wide), BF16),
+            pltpu.VMEM((tiles, peers, STEP, row_wide), BF16),
+            pltpu.VMEM((tiles, n_grp, n_sp, STEP, q_wide), BF16),
+            pltpu.VMEM((tiles, n_grp, n_sp, STEP, 2 * HEAD_DIM), BF16),
+            pltpu.VMEM((tile_tok, tile_tok), F32),
+            pltpu.VMEM((halo_tok, tile_tok), F32),
+            pltpu.VMEM((halo_tok, 2 * HEAD_DIM), BF16),
+            pltpu.VMEM((HEAD_DIM, tile_tok), BF16),
+            pltpu.VMEM((HEAD_DIM, halo_tok), BF16),
+            pltpu.VMEM((tiles, tile_tok, 2 * HEAD_DIM), F32),
+            pltpu.VMEM((halo_tok, 2 * HEAD_DIM), F32),
+            dma((parts,)),
+            dma((parts,)),
+            dma((tiles,)),
+            dma((parts,)),
+            dma((parts,)),
+            dma((parts,)),
+            dma((tiles,)),
+            dma((tiles,)),
+            dma((tiles,)),
+        ],
+        compiler_params=pltpu.CompilerParams(
+            collective_id=0, has_side_effects=True, vmem_limit_bytes=56 * 1024 * 1024
+        ),
+    )(
+        q_src.reshape(units, q_all),
+        k_src.reshape(units, kv_all),
+        v_src.reshape(units, kv_all),
+        grad_src.reshape(units, q_all),
+        doc_lengths.reshape(1, slots),
+        doc_groups.reshape(1, slots),
+        doc_offsets.reshape(1, slots),
+    )
+    rows = cap * n_grp
+    out_rows = n_grp * STEP
+    dq, dk, dv = pl.pallas_call(
+        weave_kernel,
+        grid=(tiles,),
+        out_shape=(
+            jax.ShapeDtypeStruct((rows, q_all), BF16),
+            jax.ShapeDtypeStruct((rows, kv_all), BF16),
+            jax.ShapeDtypeStruct((rows, kv_all), BF16),
+        ),
+        in_specs=[
+            pl.BlockSpec((None, n_grp, n_sp, STEP, q_wide), lambda t: (t, 0, 0, 0, 0)),
+            pl.BlockSpec((None, n_grp, n_sp, STEP, 2 * HEAD_DIM), lambda t: (t, 0, 0, 0, 0)),
+        ],
+        out_specs=(
+            pl.BlockSpec((out_rows, q_all), lambda t: (t, 0)),
+            pl.BlockSpec((out_rows, kv_all), lambda t: (t, 0)),
+            pl.BlockSpec((out_rows, kv_all), lambda t: (t, 0)),
+        ),
+        compiler_params=pltpu.CompilerParams(vmem_limit_bytes=56 * 1024 * 1024),
+    )(back_q, back_kv)
+    return (
+        dq.reshape(1, rows, 1, q_all),
+        dk.reshape(1, rows, 1, kv_all),
+        dv.reshape(1, rows, 1, kv_all),
+    )
+
+
+def on_device(q_src, k_src, v_src, grad_src, doc_lengths, doc_groups, doc_offsets):
+    n_grp = lax.axis_size("grp")
+    cap = doc_lengths.shape[0] // n_grp
+    fits = lax.axis_size("sp") == KV_HEADS and cap % STEP == 0
+    chosen = on_device_fused if fits else on_device_wide
+    return chosen(q_src, k_src, v_src, grad_src, doc_lengths, doc_groups, doc_offsets)
+
+
 def solution(mesh):
     placed = (
         P(None, "grp", "sp", None),

time: 413 us -> 114 us (0.28)
  the two profiles are of different devices: /device:TPU:24 before, /device:TPU:17 now
where the time goes in v2:
time: 114 us
  Pallas kernels  113 us (99%)
    pallas_call x1, Pallas kernels, on_device_fused(): pl.pallas_call(lambda *refs: fused_kernel(n_grp, n_sp, tiles, *refs), out...  109 us
    pallas_call x1, Pallas kernels, on_device_fused(): pl.pallas_call(weave_kernel, grid=(tiles,), out_shape=(jax.ShapeDtypeStru...  4.37 us

profile of v2, /device:TPU:17, one launch (start us, length us, event | category | flops | bytes accessed | tf_op | source)
XLA Modules:
  0.0 113.9 jit_solution(12538750243084659993)
XLA Ops:
  0.6 108.9 %shard_map.94 = (bf16[3,4,8,16,512]{4,3,2,1,0:T(8,128)(2,1)}, bf16[3,4,8,16,256]{4,3,2,1,0:T(8,128)(2,1)}) custom-call(bf16[128,4096]{1,0:T(8,128)(2,1)} %bitcast.10, bf16[128,1024]{1,0:T(8,128)(2,1)} %bitcast.12, bf16[128,1024]{1,0:T(8,128)(2,1)} %bitcast.13, bf16[128,4096]{1,0:T(8,128)(2,1)} %bitcast.11, s32[1,192]{1,0:T(1,128)} %bitcast.14, ...), custom_call_target="tpu_custom_call" | custom-call | tf_op jit(solution)/shard_map/pallas_call | solution.py:622
  109.6 4.4 %shard_map.95 = (bf16[192,4096]{1,0:T(8,128)(2,1)}, bf16[192,1024]{1,0:T(8,128)(2,1)}, bf16[192,1024]{1,0:T(8,128)(2,1)}) custom-call(bf16[3,4,8,16,512]{4,3,2,1,0:T(8,128)(2,1)} %get-tuple-element.8.back_q, bf16[3,4,8,16,256]{4,3,2,1,0:T(8,128)(2,1)} %get-tuple-element.9.back_kv), custom_call_target="tpu_custom_call" | custom-call | tf_op jit(solution)/shard_map/pallas_call | solution.py:666

commit v3 on v2

--- a/solution.py
+++ b/solution.py
@@ -294,6 +294,7 @@
     n_grp,
     n_sp,
     tiles,
+    full_grps,
     q_ref,
     k_ref,
     v_ref,
@@ -301,12 +302,15 @@
     len_ref,
     grp_ref,
     off_ref,
-    back_q,
-    back_kv,
+    dq_ref,
+    dk_ref,
+    dv_ref,
     send,
     recv,
     home_q,
-    home_kv,
+    home_k,
+    home_v,
+    order,
     bias,
     halo_bias,
     halo_kv,
@@ -320,9 +324,12 @@
     hq_send,
     hq_recv,
     hq_own,
-    hkv_send,
-    hkv_recv,
-    hkv_own,
+    hk_send,
+    hk_recv,
+    hk_own,
+    hv_send,
+    hv_recv,
+    hv_own,
 ):
     my_grp = lax.axis_index("grp")
     my_sp = lax.axis_index("sp")
@@ -384,24 +391,29 @@
                 put(to, 2 * HEAD_DIM * (head + 1), q_ref, lane, HEAD_DIM)
                 put(to, 2 * HEAD_DIM * (head + 1) + HEAD_DIM, g_ref, lane, HEAD_DIM)
 
+    def push(tile, lanes, sem, to_grp, to_sp):
+        pltpu.make_async_remote_copy(
+            src_ref=send.at[tile, to_grp * n_sp + to_sp, :, lanes],
+            dst_ref=recv.at[tile, me, :, lanes],
+            send_sem=send_sem.at[sem],
+            recv_sem=recv_sem.at[sem],
+            device_id={"grp": to_grp, "sp": to_sp},
+            device_id_type=MESH,
+        ).start()
+
+    half = n_grp // 2
+
     def scatter(tile, lane, wide, sem):
-        lanes = pl.ds(lane, wide)
-
-        def push(to_grp, to_sp):
-            pltpu.make_async_remote_copy(
-                src_ref=send.at[tile, to_grp * n_sp + to_sp, :, lanes],
-                dst_ref=recv.at[tile, me, :, lanes],
-                send_sem=send_sem.at[sem],
-                recv_sem=recv_sem.at[sem],
-                device_id={"grp": to_grp, "sp": to_sp},
-                device_id_type=MESH,
-            ).start()
-
-        for turn in [n_grp // 2] + [t for t in range(1, n_grp) if t != n_grp // 2] + [0]:
-
-            @pl.loop(1 if turn == 0 else 0, n_sp)
-            def _(hop):
-                push(lax.rem(my_grp + turn, n_grp), lax.rem(my_sp + hop, n_sp))
+        @pl.loop(0, peers)
+        def _(hop):
+            turn = hop // n_sp
+            side = lax.rem(my_grp // half + 1 + turn // half, 2)
+            to_grp = side * half + lax.rem(my_grp + turn, half)
+            to_sp = lax.rem(my_sp + hop, n_sp)
+
+            @pl.when((to_grp != my_grp) | (to_sp != my_sp))
+            def _():
+                push(tile, pl.ds(lane, wide), sem, to_grp, to_sp)
 
     def landed(tile, lane, wide, sem):
         block = recv.at[tile, pl.ds(0, peers - 1), :, pl.ds(lane, wide)]
@@ -410,46 +422,75 @@
     def own_block(tile):
         return pltpu.make_async_copy(send.at[tile, me], recv.at[tile, me], own_sem.at[tile])
 
+    pair = 2 * HEAD_DIM
+    takes_last = sum(((my_grp == grp).astype(jnp.int32) for grp in full_grps), jnp.int32(0)) > 0
+
+    pack(last)
+    pl.semaphore_wait(barrier, peers - 1)
+    if len(full_grps) == n_grp:
+        scatter(last, 0, row_wide, last)
+    else:
+        for to_grp in full_grps:
+
+            @pl.loop(0, n_sp)
+            def _(hop):
+                @pl.when((my_grp != to_grp) | (hop > 0))
+                def _():
+                    push(last, pl.ds(0, row_wide), last, to_grp, lax.rem(my_sp + hop, n_sp))
+
+    for tile in range(last - 1, 0, -1):
+        pack(tile)
+        scatter(tile, 0, row_wide, tile)
     pack(0)
-    pl.semaphore_wait(barrier, peers - 1)
+    scatter(0, 0, pair, 0)
+    for head in range(heads):
+        scatter(0, (head + 1) * pair, pair, tiles + head)
     for tile in range(last):
-        if tile > 0:
-            pack(tile)
-        scatter(tile, 0, row_wide, tile)
-    pack(last)
-    pair = 2 * HEAD_DIM
-    scatter(last, 0, 2 * pair, last)
-    for head in range(1, heads):
-        scatter(last, (head + 1) * pair, pair, last + head)
-    for tile in range(tiles):
         own_block(tile).start()
 
+    @pl.when(takes_last)
+    def _():
+        own_block(last).start()
+
+    @pl.when(jnp.logical_not(takes_last))
+    def _():
+        recv[last] = jnp.zeros(recv.shape[1:], BF16)
+
     d_acc[...] = jnp.zeros_like(d_acc)
-
-    def go_home(here, back, sends, recvs, own):
+    to_row = row_iota(tile_tok, 1)
+    out_rows = n_grp * STEP
+    of_row = (
+        (lax.rem(to_row, n_grp) * n_sp + to_row // out_rows) * STEP + lax.rem(to_row, out_rows) // n_grp
+    )
+    order[...] = (of_row == lane_iota(1, tile_tok)).astype(F32).astype(BF16)
+
+    def go_home(here, out, tile, lane, sends, recvs, own):
+        wide = here.shape[-1]
+        there = out.at[pl.ds(tile * out_rows, out_rows), pl.ds(pl.multiple_of(lane, HEAD_DIM), wide)]
+
         @pl.loop(1, n_sp)
         def _(hop):
             to_sp = lax.rem(my_sp + hop, n_sp)
             pltpu.make_async_remote_copy(
-                src_ref=here.at[:, to_sp],
-                dst_ref=back.at[:, my_sp],
+                src_ref=here.at[to_sp],
+                dst_ref=there,
                 send_sem=sends,
                 recv_sem=recvs,
                 device_id={"grp": my_grp, "sp": to_sp},
                 device_id_type=MESH,
             ).start()
 
-        pltpu.make_async_copy(here.at[:, my_sp], back.at[:, my_sp], own).start()
+        pltpu.make_async_copy(here.at[my_sp], there, own).start()
 
     def kv_home(tile):
-        shape = (n_grp, n_sp, STEP, HEAD_DIM)
-        home_kv[tile, :, :, :, :HEAD_DIM] = (
-            (d_acc[tile, :, :HEAD_DIM] * factor).astype(BF16).reshape(shape)
-        )
-        home_kv[tile, :, :, :, HEAD_DIM:] = d_acc[tile, :, HEAD_DIM:].astype(BF16).reshape(shape)
-        go_home(
-            home_kv.at[tile], back_kv.at[tile], hkv_send.at[tile], hkv_recv.at[tile], hkv_own.at[tile]
-        )
+        shape = (n_sp, out_rows, HEAD_DIM)
+        d_key = (d_acc[tile, :, :HEAD_DIM] * factor).astype(BF16)
+        home_k[tile] = dot_nn(order[...], d_key).astype(BF16).reshape(shape)
+        lane = my_sp * HEAD_DIM
+        go_home(home_k.at[tile], dk_ref, tile, lane, hk_send.at[tile], hk_recv.at[tile], hk_own.at[tile])
+        d_val = d_acc[tile, :, HEAD_DIM:].astype(BF16)
+        home_v[tile] = dot_nn(order[...], d_val).astype(BF16).reshape(shape)
+        go_home(home_v.at[tile], dv_ref, tile, lane, hv_send.at[tile], hv_recv.at[tile], hv_own.at[tile])
 
     halo_row = row_iota(halo_tok, 1)
     halo_from = (halo_row // halo) * STEP + STEP - halo + lax.rem(halo_row, halo)
@@ -460,7 +501,12 @@
         row == (halo_lane // halo) * STEP + STEP - halo + lax.rem(halo_lane, halo)
     ).astype(F32)
 
-    for tile in range(tiles):
+    @pl.when(takes_last)
+    def _():
+        own_block(last).wait()
+        landed(last, 0, row_wide, last)
+
+    for tile in range(last, -1, -1):
         lane = lane_iota(1, tile_tok)
         q_block = tile * STEP + lax.rem(lane, STEP)
         q_pos = q_block * peers + lane // STEP
@@ -477,6 +523,8 @@
         k_pos = (tile * STEP + lax.rem(row, STEP)) * peers + row // STEP
         bias[...] = jnp.where((k_pos <= q_pos) & (k_pos >= first), 0.0, NEG_FILL)
         if tile > 0:
+            own_block(tile - 1).wait()
+            landed(tile - 1, 0, row_wide if tile > 1 else pair, tile - 1)
             halo_pos = (tile * STEP - halo + lax.rem(halo_row, halo)) * peers + halo_row // halo
             halo_bias[...] = jnp.where(halo_pos >= first, 0.0, NEG_FILL)
             kv_before = recv[tile - 1, :, :, : 2 * HEAD_DIM].reshape(tile_tok, 2 * HEAD_DIM)
@@ -485,19 +533,14 @@
             halo_turned[...] = kv_cut[:, :HEAD_DIM].T.astype(BF16)
             halo_acc[...] = jnp.zeros_like(halo_acc)
 
-        own_block(tile).wait()
-        landed(tile, 0, 2 * pair if tile == last else row_wide, tile)
         k_turned[...] = (
             recv[tile, :, :, :HEAD_DIM].reshape(tile_tok, HEAD_DIM).astype(F32).T.astype(BF16)
         )
 
         @pl.loop(0, heads)
         def _(head):
-            if tile == last:
-
-                @pl.when(head > 0)
-                def _():
-                    landed(last, pair, pair, last + head)
+            if tile == 0:
+                landed(0, pair, pair, tiles + head)
 
             at = pl.multiple_of(head * HEAD_DIM, HEAD_DIM)
             q_at = pl.multiple_of((head + 1) * pair, HEAD_DIM)
@@ -537,22 +580,31 @@
                     halo_acc[:, :HEAD_DIM] += d_key
                     halo_acc[:, HEAD_DIM:] += d_val
                 dq_turned += dot_nn(turned[n][...], d_logits)
-            dq_head = (dq_turned * factor).T.astype(BF16)
+            dq_head = dot_nt(order[...], (dq_turned * factor).astype(BF16)).astype(BF16)
             lanes = pl.ds(at, HEAD_DIM)
-            home_q[tile, :, :, :, lanes] = dq_head.reshape(n_grp, n_sp, STEP, HEAD_DIM)
-            if tile == last:
+            home_q[tile, :, :, lanes] = dq_head.reshape(n_sp, out_rows, HEAD_DIM)
+            if tile == 0:
                 go_home(
-                    home_q.at[tile, :, :, :, lanes],
-                    back_q.at[tile, :, :, :, lanes],
+                    home_q.at[0, :, :, lanes],
+                    dq_ref,
+                    0,
+                    my_sp * q_wide + head * HEAD_DIM,
                     hq_send.at[last + head],
                     hq_recv.at[last + head],
                     hq_own.at[last + head],
                 )
 
-        if tile < last:
+        if tile > 0:
             go_home(
-                home_q.at[tile], back_q.at[tile], hq_send.at[tile], hq_recv.at[tile], hq_own.at[tile]
+                home_q.at[tile],
+                dq_ref,
+                tile,
+                my_sp * q_wide,
+                hq_send.at[tile - 1],
+                hq_recv.at[tile - 1],
+                hq_own.at[tile - 1],
             )
+        kv_home(tile)
         if tile > 0:
             d_acc[tile - 1] += lax.dot_general(
                 paste,
@@ -561,42 +613,63 @@
                 precision=lax.Precision.HIGHEST,
                 preferred_element_type=F32,
             )
-            kv_home(tile - 1)
-    kv_home(last)
 
     def settle(block, sem):
         pltpu.make_async_copy(block, block, sem).wait()
 
-    away = pl.ds(0, n_sp - 1)
+    def settle_home(here, sends, recvs, own):
+        away = here.at[pl.ds(0, n_sp - 1)]
+        settle(here.at[0], own)
+        settle(away, sends)
+        settle(away, recvs)
+
+    def settle_sent(tile, lane, wide, count, sem):
+        settle(send.at[tile, pl.ds(0, count), :, pl.ds(lane, wide)], send_sem.at[sem])
+
     for tile in range(tiles):
-        settle(home_kv.at[tile, :, 0], hkv_own.at[tile])
-        settle(home_kv.at[tile, :, away], hkv_send.at[tile])
-        settle(home_kv.at[tile, :, away], hkv_recv.at[tile])
-    for tile in range(last):
-        settle(home_q.at[tile, :, 0], hq_own.at[tile])
-        settle(home_q.at[tile, :, away], hq_send.at[tile])
-        settle(home_q.at[tile, :, away], hq_recv.at[tile])
-        settle(send.at[tile, pl.ds(0, peers - 1)], send_sem.at[tile])
+        settle_home(home_k.at[tile], hk_send.at[tile], hk_recv.at[tile], hk_own.at[tile])
+        settle_home(home_v.at[tile], hv_send.at[tile], hv_recv.at[tile], hv_own.at[tile])
+    for n in range(last):
+        settle_home(home_q.at[n + 1], hq_send.at[n], hq_recv.at[n], hq_own.at[n])
     for head in range(heads):
-        settle(home_q.at[last, :, 0, :, :HEAD_DIM], hq_own.at[last + head])
-        settle(home_q.at[last, :, away, :, :HEAD_DIM], hq_send.at[last + head])
-        settle(home_q.at[last, :, away, :, :HEAD_DIM], hq_recv.at[last + head])
-        wide = 2 * pair if head == 0 else pair
-        settle(send.at[last, pl.ds(0, peers - 1), :, :wide], send_sem.at[last + head])
-
-
-def weave_kernel(back_q, back_kv, dq_ref, dk_ref, dv_ref):
-    n_grp, n_sp, step, q_wide = back_q.shape
-    rows = n_grp * step
-    from_row = lane_iota(rows, rows)
-    weave = row_iota(rows, rows) == lax.rem(from_row, step) * n_grp + from_row // step
-    weave = weave.astype(F32).astype(BF16)
-    for sp in range(n_sp):
-        part = dot_nn(weave, back_q[:, sp].reshape(rows, q_wide)).astype(BF16)
-        dq_ref[:, sp * q_wide : (sp + 1) * q_wide] = part
-        both = dot_nn(weave, back_kv[:, sp].reshape(rows, 2 * HEAD_DIM)).astype(BF16)
-        dk_ref[:, sp * HEAD_DIM : (sp + 1) * HEAD_DIM] = both[:, :HEAD_DIM]
-        dv_ref[:, sp * HEAD_DIM : (sp + 1) * HEAD_DIM] = both[:, HEAD_DIM:]
+        n = last + head
+        settle_home(home_q.at[0, :, :, pl.ds(0, HEAD_DIM)], hq_send.at[n], hq_recv.at[n], hq_own.at[n])
+        settle_sent(0, 0, pair, peers - 1, tiles + head)
+    settle_sent(0, 0, pair, peers - 1, 0)
+    for tile in range(1, last):
+        settle_sent(tile, 0, row_wide, peers - 1, tile)
+
+    @pl.when(takes_last)
+    def _():
+        settle_sent(last, 0, row_wide, len(full_grps) * n_sp - 1, last)
+
+    if len(full_grps) < n_grp:
+
+        @pl.when(jnp.logical_not(takes_last))
+        def _():
+            settle_sent(last, 0, row_wide, len(full_grps) * n_sp, last)
+
+
+def result_kernel(*refs):
+    sources, results, held = refs[:3], refs[3:6], refs[6:9]
+    load_sem, store_sem = refs[9:]
+    rows = held[0].shape[0]
+    cuts = [(0, pl.ds(n * rows // 4, rows // 4)) for n in range(4)] + [(1, pl.ds(0, rows)), (2, pl.ds(0, rows))]
+    loads = [
+        pltpu.make_async_copy(sources[n].at[cut], held[n].at[cut], load_sem.at[i])
+        for i, (n, cut) in enumerate(cuts)
+    ]
+    stores = [
+        pltpu.make_async_copy(held[n].at[cut], results[n].at[cut], store_sem.at[i])
+        for i, (n, cut) in enumerate(cuts)
+    ]
+    for load in loads:
+        load.start()
+    for load, store in zip(loads, stores):
+        load.wait()
+        store.start()
+    for store in stores:
+        store.wait()
 
 
 def on_device_fused(q_src, k_src, v_src, grad_src, doc_lengths, doc_groups, doc_offsets):
@@ -614,74 +687,67 @@
     row_wide = 2 * HEAD_DIM * (heads + 1)
     tile_tok = peers * STEP
     halo_tok = peers * (MAXDOC - 1)
-    parts = tiles - 1 + heads
-
+    out_rows = n_grp * STEP
+    rows = cap * n_grp
+    shapes = (
+        jax.ShapeDtypeStruct((rows, q_all), BF16),
+        jax.ShapeDtypeStruct((rows, kv_all), BF16),
+        jax.ShapeDtypeStruct((rows, kv_all), BF16),
+    )
     vmem = pl.BlockSpec(memory_space=pltpu.VMEM)
     hbm = pl.BlockSpec(memory_space=pl.ANY)
     dma = pltpu.SemaphoreType.DMA
-    back_q, back_kv = pl.pallas_call(
-        lambda *refs: fused_kernel(n_grp, n_sp, tiles, *refs),
-        out_shape=(
-            jax.ShapeDtypeStruct((tiles, n_grp, n_sp, STEP, q_wide), BF16),
-            jax.ShapeDtypeStruct((tiles, n_grp, n_sp, STEP, 2 * HEAD_DIM), BF16),
-        ),
-        in_specs=[vmem] * 7,
-        out_specs=(hbm, hbm),
-        scratch_shapes=[
-            pltpu.VMEM((tiles, peers, STEP, row_wide), BF16),
-            pltpu.VMEM((tiles, peers, STEP, row_wide), BF16),
-            pltpu.VMEM((tiles, n_grp, n_sp, STEP, q_wide), BF16),
-            pltpu.VMEM((tiles, n_grp, n_sp, STEP, 2 * HEAD_DIM), BF16),
-            pltpu.VMEM((tile_tok, tile_tok), F32),
-            pltpu.VMEM((halo_tok, tile_tok), F32),
-            pltpu.VMEM((halo_tok, 2 * HEAD_DIM), BF16),
-            pltpu.VMEM((HEAD_DIM, tile_tok), BF16),
-            pltpu.VMEM((HEAD_DIM, halo_tok), BF16),
-            pltpu.VMEM((tiles, tile_tok, 2 * HEAD_DIM), F32),
-            pltpu.VMEM((halo_tok, 2 * HEAD_DIM), F32),
-            dma((parts,)),
-            dma((parts,)),
-            dma((tiles,)),
-            dma((parts,)),
-            dma((parts,)),
-            dma((parts,)),
-            dma((tiles,)),
-            dma((tiles,)),
-            dma((tiles,)),
-        ],
-        compiler_params=pltpu.CompilerParams(
-            collective_id=0, has_side_effects=True, vmem_limit_bytes=56 * 1024 * 1024
-        ),
-    )(
-        q_src.reshape(units, q_all),
-        k_src.reshape(units, kv_all),
-        v_src.reshape(units, kv_all),
-        grad_src.reshape(units, q_all),
-        doc_lengths.reshape(1, slots),
-        doc_groups.reshape(1, slots),
-        doc_offsets.reshape(1, slots),
-    )
-    rows = cap * n_grp
-    out_rows = n_grp * STEP
+
+    def run(full_grps, number):
+        return pl.pallas_call(
+            lambda *refs: fused_kernel(n_grp, n_sp, tiles, full_grps, *refs),
+            out_shape=shapes,
+            in_specs=[vmem] * 7,
+            out_specs=(hbm,) * 3,
+            scratch_shapes=[
+                pltpu.VMEM((tiles, peers, STEP, row_wide), BF16),
+                pltpu.VMEM((tiles, peers, STEP, row_wide), BF16),
+                pltpu.VMEM((tiles, n_sp, out_rows, q_wide), BF16),
+                pltpu.VMEM((tiles, n_sp, out_rows, HEAD_DIM), BF16),
+                pltpu.VMEM((tiles, n_sp, out_rows, HEAD_DIM), BF16),
+                pltpu.VMEM((tile_tok, tile_tok), BF16),
+                pltpu.VMEM((tile_tok, tile_tok), F32),
+                pltpu.VMEM((halo_tok, tile_tok), F32),
+                pltpu.VMEM((halo_tok, 2 * HEAD_DIM), BF16),
+                pltpu.VMEM((HEAD_DIM, tile_tok), BF16),
+                pltpu.VMEM((HEAD_DIM, halo_tok), BF16),
+                pltpu.VMEM((tiles, tile_tok, 2 * HEAD_DIM), F32),
+                pltpu.VMEM((halo_tok, 2 * HEAD_DIM), F32),
+                dma((tiles + heads,)),
+                dma((tiles + heads,)),
+                dma((tiles,)),
+                dma((tiles - 1 + heads,)),
+                dma((tiles - 1 + heads,)),
+                dma((tiles - 1 + heads,)),
+            ]
+            + [dma((tiles,))] * 6,
+            compiler_params=pltpu.CompilerParams(
+                collective_id=number, has_side_effects=True, vmem_limit_bytes=56 * 1024 * 1024
+            ),
+        )(
+            q_src.reshape(units, q_all),
+            k_src.reshape(units, kv_all),
+            v_src.reshape(units, kv_all),
+            grad_src.reshape(units, q_all),
+            doc_lengths.reshape(1, slots),
+            doc_groups.reshape(1, slots),
+            doc_offsets.reshape(1, slots),
+        )
+
+    passed = run(tuple(range(n_grp)), 0)
     dq, dk, dv = pl.pallas_call(
-        weave_kernel,
-        grid=(tiles,),
-        out_shape=(
-            jax.ShapeDtypeStruct((rows, q_all), BF16),
-            jax.ShapeDtypeStruct((rows, kv_all), BF16),
-            jax.ShapeDtypeStruct((rows, kv_all), BF16),
-        ),
-        in_specs=[
-            pl.BlockSpec((None, n_grp, n_sp, STEP, q_wide), lambda t: (t, 0, 0, 0, 0)),
-            pl.BlockSpec((None, n_grp, n_sp, STEP, 2 * HEAD_DIM), lambda t: (t, 0, 0, 0, 0)),
-        ],
-        out_specs=(
-            pl.BlockSpec((out_rows, q_all), lambda t: (t, 0)),
-            pl.BlockSpec((out_rows, kv_all), lambda t: (t, 0)),
-            pl.BlockSpec((out_rows, kv_all), lambda t: (t, 0)),
-        ),
+        result_kernel,
+        out_shape=shapes,
+        in_specs=[hbm] * 3,
+        out_specs=(hbm,) * 3,
+        scratch_shapes=[pltpu.VMEM(shape.shape, BF16) for shape in shapes] + [dma((6,)), dma((6,))],
         compiler_params=pltpu.CompilerParams(vmem_limit_bytes=56 * 1024 * 1024),
-    )(back_q, back_kv)
+    )(*passed)
     return (
         dq.reshape(1, rows, 1, q_all),
         dk.reshape(1, rows, 1, kv_all),
@@ -692,7 +758,7 @@
 def on_device(q_src, k_src, v_src, grad_src, doc_lengths, doc_groups, doc_offsets):
     n_grp = lax.axis_size("grp")
     cap = doc_lengths.shape[0] // n_grp
-    fits = lax.axis_size("sp") == KV_HEADS and cap % STEP == 0
+    fits = lax.axis_size("sp") == KV_HEADS and cap % STEP == 0 and cap > STEP and n_grp % 2 == 0
     chosen = on_device_fused if fits else on_device_wide
     return chosen(q_src, k_src, v_src, grad_src, doc_lengths, doc_groups, doc_offsets)
 

time: 114 us -> 120 us (1.053)
  Pallas kernels: 113 us -> 119 us
    pallas_call x2, Pallas kernels: 113 us -> 119 us  [the longest x1 116 us: run(): pl.pallas_call(lambda *refs: fused_kernel(n_grp, n_sp, tiles, full_grps,...]
where the time goes in v3:
time: 120 us
  Pallas kernels  119 us (99%)
    pallas_call x1, Pallas kernels, run(): pl.pallas_call(lambda *refs: fused_kernel(n_grp, n_sp, tiles, full_grps,...  116 us
    pallas_call x1, Pallas kernels, on_device_fused(): pl.pallas_call(result_kernel, out_shape=shapes, in_specs=[hbm] * 3, out_s...  2.49 us

profile of v3, /device:TPU:17, one launch (start us, length us, event | category | flops | bytes accessed | tf_op | source)
XLA Modules:
  0.0 119.5 jit_solution(17031784162166147171)
XLA Ops:
  0.6 116.2 %shard_map.94 = (bf16[192,4096]{1,0:T(8,128)(2,1)}, bf16[192,1024]{1,0:T(8,128)(2,1)}, bf16[192,1024]{1,0:T(8,128)(2,1)}) custom-call(bf16[128,4096]{1,0:T(8,128)(2,1)} %bitcast.10, bf16[128,1024]{1,0:T(8,128)(2,1)} %bitcast.12, bf16[128,1024]{1,0:T(8,128)(2,1)} %bitcast.13, bf16[128,4096]{1,0:T(8,128)(2,1)} %bitcast.11, s32[1,192]{1,0:T(1,128)} %bitcast.14, ...), custom_call_target="tpu_custom_call" | custom-call | tf_op jit(solution)/shard_map/pallas_call | solution.py:702
  116.9 2.5 %shard_map.95 = (bf16[192,4096]{1,0:T(8,128)(2,1)}, bf16[192,1024]{1,0:T(8,128)(2,1)}, bf16[192,1024]{1,0:T(8,128)(2,1)}) custom-call(bf16[192,4096]{1,0:T(8,128)(2,1)} %get-tuple-element.9.refs_0_, bf16[192,1024]{1,0:T(8,128)(2,1)} %get-tuple-element.10.refs_1_, bf16[192,1024]{1,0:T(8,128)(2,1)} %get-tuple-element.11.refs_2_), custom_call_target="tpu_custom_call" | custom-call | tf_op jit(solution)/shard_map/pallas_call | solution.py:743

commit v4 on v3

--- a/solution.py
+++ b/solution.py
@@ -406,10 +406,8 @@
     def scatter(tile, lane, wide, sem):
         @pl.loop(0, peers)
         def _(hop):
-            turn = hop // n_sp
-            side = lax.rem(my_grp // half + 1 + turn // half, 2)
-            to_grp = side * half + lax.rem(my_grp + turn, half)
-            to_sp = lax.rem(my_sp + hop, n_sp)
+            to_grp = lax.rem(my_grp + half + hop, n_grp)
+            to_sp = lax.rem(my_sp + hop // n_grp, n_sp)
 
             @pl.when((to_grp != my_grp) | (to_sp != my_sp))
             def _():
@@ -430,17 +428,19 @@
     if len(full_grps) == n_grp:
         scatter(last, 0, row_wide, last)
     else:
-        for to_grp in full_grps:
-
-            @pl.loop(0, n_sp)
-            def _(hop):
+
+        @pl.loop(0, n_sp)
+        def _(hop):
+            for to_grp in full_grps:
+
                 @pl.when((my_grp != to_grp) | (hop > 0))
                 def _():
                     push(last, pl.ds(0, row_wide), last, to_grp, lax.rem(my_sp + hop, n_sp))
 
     for tile in range(last - 1, 0, -1):
         pack(tile)
-        scatter(tile, 0, row_wide, tile)
+        scatter(tile, 0, pair, tile)
+        scatter(tile, pair, row_wide - pair, tiles + heads + tile)
     pack(0)
     scatter(0, 0, pair, 0)
     for head in range(heads):
@@ -523,8 +523,10 @@
         k_pos = (tile * STEP + lax.rem(row, STEP)) * peers + row // STEP
         bias[...] = jnp.where((k_pos <= q_pos) & (k_pos >= first), 0.0, NEG_FILL)
         if tile > 0:
+            if tile < last:
+                landed(tile, pair, row_wide - pair, tiles + heads + tile)
             own_block(tile - 1).wait()
-            landed(tile - 1, 0, row_wide if tile > 1 else pair, tile - 1)
+            landed(tile - 1, 0, pair, tile - 1)
             halo_pos = (tile * STEP - halo + lax.rem(halo_row, halo)) * peers + halo_row // halo
             halo_bias[...] = jnp.where(halo_pos >= first, 0.0, NEG_FILL)
             kv_before = recv[tile - 1, :, :, : 2 * HEAD_DIM].reshape(tile_tok, 2 * HEAD_DIM)
@@ -637,7 +639,8 @@
         settle_sent(0, 0, pair, peers - 1, tiles + head)
     settle_sent(0, 0, pair, peers - 1, 0)
     for tile in range(1, last):
-        settle_sent(tile, 0, row_wide, peers - 1, tile)
+        settle_sent(tile, 0, pair, peers - 1, tile)
+        settle_sent(tile, pair, row_wide - pair, peers - 1, tiles + heads + tile)
 
     @pl.when(takes_last)
     def _():
@@ -718,8 +721,8 @@
                 pltpu.VMEM((HEAD_DIM, halo_tok), BF16),
                 pltpu.VMEM((tiles, tile_tok, 2 * HEAD_DIM), F32),
                 pltpu.VMEM((halo_tok, 2 * HEAD_DIM), F32),
-                dma((tiles + heads,)),
-                dma((tiles + heads,)),
+                dma((2 * tiles + heads,)),
+                dma((2 * tiles + heads,)),
                 dma((tiles,)),
                 dma((tiles - 1 + heads,)),
                 dma((tiles - 1 + heads,)),

time: 120 us -> 114 us (0.950)
  Pallas kernels: 119 us -> 112 us
    pallas_call x1, Pallas kernels: 116 us -> 109 us  [run(): pl.pallas_call(lambda *refs: fused_kernel(n_grp, n_sp, tiles, full_grps,...]
where the time goes in v4:
time: 114 us; the launch traced here: 112 us
  Pallas kernels  112 us (98%)
    pallas_call x1, Pallas kernels, run(): pl.pallas_call(lambda *refs: fused_kernel(n_grp, n_sp, tiles, full_grps,...  109 us
    pallas_call x1, Pallas kernels, on_device_fused(): pl.pallas_call(result_kernel, out_shape=shapes, in_specs=[hbm] * 3, out_s...  2.49 us

profile of v4, /device:TPU:17, one launch (start us, length us, event | category | flops | bytes accessed | tf_op | source)
XLA Modules:
  0.0 112.4 jit_solution(17470462088310120589)
XLA Ops:
  0.6 109.1 %shard_map.94 = (bf16[192,4096]{1,0:T(8,128)(2,1)}, bf16[192,1024]{1,0:T(8,128)(2,1)}, bf16[192,1024]{1,0:T(8,128)(2,1)}) custom-call(bf16[128,4096]{1,0:T(8,128)(2,1)} %bitcast.10, bf16[128,1024]{1,0:T(8,128)(2,1)} %bitcast.12, bf16[128,1024]{1,0:T(8,128)(2,1)} %bitcast.13, bf16[128,4096]{1,0:T(8,128)(2,1)} %bitcast.11, s32[1,192]{1,0:T(1,128)} %bitcast.14, ...), custom_call_target="tpu_custom_call" | custom-call | tf_op jit(solution)/shard_map/pallas_call | solution.py:705
  109.7 2.5 %shard_map.95 = (bf16[192,4096]{1,0:T(8,128)(2,1)}, bf16[192,1024]{1,0:T(8,128)(2,1)}, bf16[192,1024]{1,0:T(8,128)(2,1)}) custom-call(bf16[192,4096]{1,0:T(8,128)(2,1)} %get-tuple-element.9.refs_0_, bf16[192,1024]{1,0:T(8,128)(2,1)} %get-tuple-element.10.refs_1_, bf16[192,1024]{1,0:T(8,128)(2,1)} %get-tuple-element.11.refs_2_), custom_call_target="tpu_custom_call" | custom-call | tf_op jit(solution)/shard_map/pallas_call | solution.py:746

commit v5 on v4

--- a/solution.py
+++ b/solution.py
@@ -404,14 +404,12 @@
     half = n_grp // 2
 
     def scatter(tile, lane, wide, sem):
-        @pl.loop(0, peers)
-        def _(hop):
-            to_grp = lax.rem(my_grp + half + hop, n_grp)
-            to_sp = lax.rem(my_sp + hop // n_grp, n_sp)
-
-            @pl.when((to_grp != my_grp) | (to_sp != my_sp))
-            def _():
-                push(tile, pl.ds(lane, wide), sem, to_grp, to_sp)
+        for turn in [half] + [t for t in range(1, n_grp) if t != half] + [0]:
+
+            @pl.loop(1 if turn == 0 else 0, n_sp)
+            def _(hop):
+                to_grp = lax.rem(my_grp + turn, n_grp)
+                push(tile, pl.ds(lane, wide), sem, to_grp, lax.rem(my_sp + hop, n_sp))
 
     def landed(tile, lane, wide, sem):
         block = recv.at[tile, pl.ds(0, peers - 1), :, pl.ds(lane, wide)]

time: 114 us -> 113 us (level); the launches traced: 112 us -> 113 us
  no operation moved by 1% of the time
where the time goes in v5:
time: 113 us
  Pallas kernels  112 us (99%)
    pallas_call x1, Pallas kernels, run(): pl.pallas_call(lambda *refs: fused_kernel(n_grp, n_sp, tiles, full_grps,...  109 us
    pallas_call x1, Pallas kernels, on_device_fused(): pl.pallas_call(result_kernel, out_shape=shapes, in_specs=[hbm] * 3, out_s...  2.49 us

profile of v5, /device:TPU:17, one launch (start us, length us, event | category | flops | bytes accessed | tf_op | source)
XLA Modules:
  0.0 112.6 jit_solution(5776720696471187427)
XLA Ops:
  0.6 109.3 %shard_map.94 = (bf16[192,4096]{1,0:T(8,128)(2,1)}, bf16[192,1024]{1,0:T(8,128)(2,1)}, bf16[192,1024]{1,0:T(8,128)(2,1)}) custom-call(bf16[128,4096]{1,0:T(8,128)(2,1)} %bitcast.10, bf16[128,1024]{1,0:T(8,128)(2,1)} %bitcast.12, bf16[128,1024]{1,0:T(8,128)(2,1)} %bitcast.13, bf16[128,4096]{1,0:T(8,128)(2,1)} %bitcast.11, s32[1,192]{1,0:T(1,128)} %bitcast.14, ...), custom_call_target="tpu_custom_call" | custom-call | tf_op jit(solution)/shard_map/pallas_call | solution.py:703
  109.9 2.5 %shard_map.95 = (bf16[192,4096]{1,0:T(8,128)(2,1)}, bf16[192,1024]{1,0:T(8,128)(2,1)}, bf16[192,1024]{1,0:T(8,128)(2,1)}) custom-call(bf16[192,4096]{1,0:T(8,128)(2,1)} %get-tuple-element.9.refs_0_, bf16[192,1024]{1,0:T(8,128)(2,1)} %get-tuple-element.10.refs_1_, bf16[192,1024]{1,0:T(8,128)(2,1)} %get-tuple-element.11.refs_2_), custom_call_target="tpu_custom_call" | custom-call | tf_op jit(solution)/shard_map/pallas_call | solution.py:744
